TPU v7x, 32 devices: a whole 2x2x4 slice. The times are simulated.
32 devices in a mesh: groups: 2 (over y), expert: 16 (over z, x, core).
Axes of the slice: x: 2, y: 2, z: 4, core: 2. Of those that a mesh axis runs over, the one named last changes fastest.
Arguments:
- tokens: bfloat16 [4096, 3584], P(('groups', 'expert')), parts along dimension 0, may hold values from -6 to 6
- gates: float32 [4096, 1], P(('groups', 'expert')), parts along dimension 0, may hold values from 0.1 to 1
- routes: int32 [4096, 1], P(('groups', 'expert')), parts along dimension 0, may hold values from 0 to 1; in each aligned block of 128 rows (0 to 127, 128 to 255, ...) at most 96 rows name the same one
- counts: int32 [32], P(('groups', 'expert')), parts along dimension 0, may hold values from 64 to 128, as said below
- w_gate: bfloat16 [16, 1792, 256], P('expert'), may hold values from -0.09375 to 0.09375
- w_up: bfloat16 [16, 1792, 256], P('expert'), may hold values from -0.09375 to 0.09375
- w_down: bfloat16 [16, 256, 1792], P('expert'), may hold values from -0.1875 to 0.1875
- cotangent: bfloat16 [4096, 3584], P(('groups', 'expert')), parts along dimension 0, may hold values from -6 to 6
Outputs:
- mixed: bfloat16 [4096, 3584], P(('groups', 'expert')), parts along dimension 0
- grad_tokens: bfloat16 [4096, 3584], P(('groups', 'expert')), parts along dimension 0
- grad_gates: float32 [4096, 1], P(('groups', 'expert')), parts along dimension 0
- grad_w_gate: bfloat16 [32, 1792, 256], P(('groups', 'expert')), parts along dimension 0
- grad_w_up: bfloat16 [32, 1792, 256], P(('groups', 'expert')), parts along dimension 0
- grad_w_down: bfloat16 [32, 256, 1792], P(('groups', 'expert')), parts along dimension 0
There are 2 independent parts, one for each index of `groups`. A program takes and returns all parts, laid end to end along the dimension named above; an argument that names none is the same for every part. Nothing has to cross between parts.
Inputs may be any that keep to these rules, and one draw needn't show every extreme that they name: `routes`: among the 128 rows of one device, no expert is named in more than 96 pairs, and some expert is named in exactly 96 pairs. `counts`: in every draw some device has all 128 slots live.
All inputs are finite; a program needn't handle non-finite values.
Results may differ from a plain program's by a relative error of at most 0.015.
Values may be sent and summed in bfloat16 or wider, within the bound.
A program may use at most 128 MiB of HBM per device.

v0:
```python
import jax
import jax.numpy as jnp
from jax import lax
from jax.sharding import PartitionSpec as P


def from_partner(value, axis, distance):
    mask = 2**distance
    pairs = [(source, source ^ mask) for source in range(lax.axis_size(axis))]
    return lax.ppermute(value, axis, pairs)


def forward_rows(rows, wg, wu, wd):
    g_part = jnp.dot(rows, wg, preferred_element_type=jnp.float32)
    u_part = jnp.dot(rows, wu, preferred_element_type=jnp.float32)
    stacked = jnp.stack([g_part, u_part])
    partner = from_partner(stacked.astype(jnp.bfloat16), "expert", 0).astype(stacked.dtype)
    total = stacked + partner
    g = total[0]
    u = total[1]
    sg = jax.nn.sigmoid(g)
    act = (g * sg * u).astype(jnp.bfloat16)
    out_part = jnp.dot(act, wd, preferred_element_type=jnp.float32).astype(jnp.bfloat16)
    return (g, u, sg, act, out_part)


def backward_rows(rows, scaled, saved, wg, wu, wd):
    g, u, sg, act, unused_out = saved
    last_last = (((1,), (1,)), ((), ()))
    first_first = (((0,), (0,)), ((), ()))
    act_part = lax.dot_general(scaled, wd, last_last, preferred_element_type=jnp.float32)
    d_act = act_part + from_partner(act_part.astype(jnp.bfloat16), "expert", 0).astype(
        act_part.dtype
    )
    grad_wd = lax.dot_general(act, scaled, first_first, preferred_element_type=jnp.float32)
    d_gate = (d_act * u * sg * (1.0 + g * (1.0 - sg))).astype(jnp.bfloat16)
    d_up = (d_act * g * sg).astype(jnp.bfloat16)
    grad_wg = lax.dot_general(rows, d_gate, first_first, preferred_element_type=jnp.float32)
    grad_wu = lax.dot_general(rows, d_up, first_first, preferred_element_type=jnp.float32)
    d_row = lax.dot_general(d_gate, wg, last_last, preferred_element_type=jnp.float32)
    d_row = d_row + lax.dot_general(d_up, wu, last_last, preferred_element_type=jnp.float32)
    return (grad_wg, grad_wu, grad_wd, d_row.astype(jnp.bfloat16))


def on_device(tokens, gates, routes, counts, w_gate, w_up, w_down, cotangent):
    peers = lax.axis_size("expert")
    tok_rows, topk = routes.shape
    width = tokens.shape[1]
    half = width // 2
    experts = peers // 8
    capacity = max(2, 3 * tok_rows * topk // (2 * experts))
    flat_n = tok_rows * topk
    valid = jnp.arange(tok_rows, dtype=jnp.int32) < counts[0]
    target = jnp.where(valid[:, None], routes, experts).reshape(flat_n)
    onehot = (target[:, None] == jnp.arange(experts, dtype=jnp.int32)[None, :]).astype(jnp.int32)
    running = jnp.cumsum(onehot, axis=0)
    slot_pos = jnp.sum((running - 1) * onehot, axis=1)
    owner = jnp.arange(flat_n, dtype=jnp.int32) // topk
    gate_flat = gates.reshape(flat_n)
    cot_rows = cotangent[owner].astype(jnp.float32)
    scaled = (gate_flat[:, None] * cot_rows).astype(jnp.bfloat16)
    empty = jnp.zeros((experts, 2, capacity, half), jnp.bfloat16)
    by_expert_x = empty.at[target, :, slot_pos].set(
        tokens[owner].reshape(flat_n, 2, half), mode="drop"
    )
    by_expert_grad = empty.at[target, :, slot_pos].set(scaled.reshape(flat_n, 2, half), mode="drop")

    def pack(by_expert):
        return jnp.broadcast_to(by_expert[:, None], (experts, 4, 2, capacity, half)).reshape(
            peers, capacity, half
        )

    def unpack(returned):
        return jnp.sum(
            returned.reshape(experts, 4, 2, capacity, half).astype(jnp.float32), axis=1
        ).astype(jnp.bfloat16)

    wg, wu, wd = (w_gate[0], w_up[0], w_down[0])
    recv_x, recv_grad = (
        lax.all_to_all(pack(by_expert_x), "expert", split_axis=0, concat_axis=0, tiled=True),
        lax.all_to_all(pack(by_expert_grad), "expert", split_axis=0, concat_axis=0, tiled=True),
    )
    received = jnp.stack([recv_x, recv_grad])
    lead = received.shape[:-3]
    both_rows = received.reshape(lead + (peers * capacity, half))
    rows = both_rows[0]
    saved = forward_rows(rows, wg, wu, wd)
    grad_wg, grad_wu, grad_wd, d_row = backward_rows(rows, both_rows[1], saved, wg, wu, wd)
    partial_value = jnp.stack([saved[4], d_row])
    lead = partial_value.shape[:-2]
    shaped = partial_value.reshape(lead + (peers, capacity, half))
    back_out, back_dx = (
        lax.all_to_all(shaped[0], "expert", split_axis=0, concat_axis=0, tiled=True),
        lax.all_to_all(shaped[1], "expert", split_axis=0, concat_axis=0, tiled=True),
    )
    summed_out = unpack(back_out)
    summed_dx = unpack(back_dx)
    keep = (target < experts)[:, None]
    safe_target = jnp.minimum(target, experts - 1)
    out_rows = jnp.where(
        keep, summed_out[safe_target, :, slot_pos].reshape(flat_n, width).astype(jnp.float32), 0.0
    )
    dx_rows = jnp.where(
        keep, summed_dx[safe_target, :, slot_pos].reshape(flat_n, width).astype(jnp.float32), 0.0
    )
    mixed = jnp.sum((gate_flat[:, None] * out_rows).reshape(tok_rows, topk, width), axis=1).astype(
        jnp.bfloat16
    )
    grad_tokens = jnp.sum(dx_rows.reshape(tok_rows, topk, width), axis=1).astype(jnp.bfloat16)
    grad_gates = jnp.sum(cot_rows * out_rows, axis=1).reshape(tok_rows, topk)
    return (
        mixed,
        grad_tokens,
        grad_gates,
        grad_wg.astype(jnp.bfloat16)[None],
        grad_wu.astype(jnp.bfloat16)[None],
        grad_wd.astype(jnp.bfloat16)[None],
    )


def solution(mesh):
    in_specs = (
        P(("groups", "expert"), None),
        P(("groups", "expert"), None),
        P(("groups", "expert"), None),
        P(("groups", "expert")),
        P("expert", None, None),
        P("expert", None, None),
        P("expert", None, None),
        P(("groups", "expert"), None),
    )
    out_specs = (
        P(("groups", "expert"), None),
        P(("groups", "expert"), None),
        P(("groups", "expert"), None),
        P(("groups", "expert"), None, None),
        P(("groups", "expert"), None, None),
        P(("groups", "expert"), None, None),
    )
    return jax.shard_map(
        on_device, mesh=mesh, in_specs=in_specs, out_specs=out_specs, check_vma=False
    )
```

profile of v0, /device:TPU:8, one launch (start us, length us, event | category | flops | bytes accessed | tf_op | source)
XLA Modules:
  0.0 536.8 jit_solution(17696863258102911367)
XLA Ops:
  2.5 3.3 gather_fusion
  6.8 6.1 %scatter_fusion = bf16[2,2,96,1792]{3,1,2,0:T(2,128)(2,1)S(1)} fusion(bf16[2,2,96,1792]{3,1,2,0:T(2,128)(2,1)S(1)} %broadcast_in_dim.62.clone, s32[128]{0:T(128)S(1)} %get-tuple-element.13, bf16[128,2,1792]{2,1,0:T(2,128)(2,1)S(1)} %reshape.164), kind=kCustom, calls=%fused_computation.4 | custom fusion | bytes 2753536 | tf_op jit(solution)/shard_map/scatter | solution.py:63
  13.0 3.0 broadcast_in_dim.63
  16.0 6.3 %all-to-all-start = ((bf16[16,96,1792]{2,1,0:T(8,128)(2,1)}), bf16[16,96,1792]{2,1,0:T(8,128)(2,1)}, u32[]{:S(2)}, u32[]{:S(2)}) async-start(bf16[16,96,1792]{2,1,0:T(8,128)(2,1)} %bitcast.108), calls=%async_computation | async-start | bytes 11010048 | tf_op jit(solution)/shard_map/all_to_all | solution.py:80
  23.5 2.5 reshape.132
  26.0 3.1 multiply_convert_fusion
  29.8 13.0 %scatter_fusion.1 = bf16[2,2,96,1792]{3,1,2,0:T(2,128)(2,1)S(1)} fusion(bf16[2,2,96,1792]{3,1,2,0:T(2,128)(2,1)S(1)} %broadcast_in_dim.62.clone.1, s32[128]{0:T(128)S(1)} %get-tuple-element.13, bf16[128,2,1792]{2,1,0:T(2,128)(2,1)} %multiply_convert_fusion), kind=kCustom, calls=%fused_computation.5 | custom fusion | bytes 2753536 | tf_op jit(solution)/shard_map/scatter | solution.py:66
  44.1 97.2 %all-to-all-done = bf16[16,96,1792]{2,1,0:T(8,128)(2,1)} async-done(((bf16[16,96,1792]{2,1,0:T(8,128)(2,1)}), bf16[16,96,1792]{2,1,0:T(8,128)(2,1)}, u32[]{:S(2)}, u32[]{:S(2)}) %all-to-all-start) | async-done | bytes 5505056 | tf_op jit(solution)/shard_map/all_to_all | solution.py:80
  141.3 4.2 broadcast_in_dim.65
  145.5 6.7 %all-to-all-start.2 = ((bf16[16,96,1792]{2,1,0:T(8,128)(2,1)}), bf16[16,96,1792]{2,1,0:T(8,128)(2,1)}, u32[]{:S(2)}, u32[]{:S(2)}) async-start(bf16[16,96,1792]{2,1,0:T(8,128)(2,1)} %bitcast.107), calls=%async_computation.2 | async-start | bytes 11010048 | tf_op jit(solution)/shard_map/all_to_all | solution.py:81
  152.2 4.3 convolution_bitcast_fusion
  156.5 4.2 convolution_bitcast_fusion.1
  161.2 3.3 collective-permute-done
  167.1 4.0 convolution_convert_fusion
  171.1 100.0 %all-to-all-done.2 = bf16[16,96,1792]{2,1,0:T(8,128)(2,1)} async-done(((bf16[16,96,1792]{2,1,0:T(8,128)(2,1)}), bf16[16,96,1792]{2,1,0:T(8,128)(2,1)}, u32[]{:S(2)}, u32[]{:S(2)}) %all-to-all-start.2) | async-done | bytes 5505056 | tf_op jit(solution)/shard_map/all_to_all | solution.py:81
  271.1 6.6 %all-to-all-start.1 = ((bf16[16,96,1792]{2,1,0:T(8,128)(2,1)}), bf16[16,96,1792]{2,1,0:T(8,128)(2,1)}, u32[]{:S(2)}, u32[]{:S(2)}) async-start(bf16[16,96,1792]{2,1,0:T(8,128)(2,1)} %bitcast.105), calls=%async_computation.1 | async-start | bytes 11010048 | tf_op jit(solution)/shard_map/all_to_all | solution.py:93
  277.7 4.4 fusion.30
  282.3 2.1 collective-permute-done.1
  287.2 4.0 add_convert_fusion
  291.2 105.3 %all-to-all-done.1 = bf16[16,96,1792]{2,1,0:T(8,128)(2,1)} async-done(((bf16[16,96,1792]{2,1,0:T(8,128)(2,1)}), bf16[16,96,1792]{2,1,0:T(8,128)(2,1)}, u32[]{:S(2)}, u32[]{:S(2)}) %all-to-all-start.1) | async-done | bytes 5505056 | tf_op jit(solution)/shard_map/all_to_all | solution.py:93
  396.6 6.6 %all-to-all-start.3 = ((bf16[16,96,1792]{2,1,0:T(8,128)(2,1)}), bf16[16,96,1792]{2,1,0:T(8,128)(2,1)}, u32[]{:S(2)}, u32[]{:S(2)}) async-start(bf16[16,96,1792]{2,1,0:T(8,128)(2,1)} %bitcast.106), calls=%async_computation.3 | async-start | bytes 11010048 | tf_op jit(solution)/shard_map/all_to_all | solution.py:94
  403.1 5.2 fusion.3
  408.3 5.1 fusion.2
  413.4 5.1 fusion.1
  418.6 3.6 reduce_sum.54
  422.1 2.5 copy.19
  424.7 3.9 gather_fusion.1
  430.0 92.0 %all-to-all-done.3 = bf16[16,96,1792]{2,1,0:T(8,128)(2,1)} async-done(((bf16[16,96,1792]{2,1,0:T(8,128)(2,1)}), bf16[16,96,1792]{2,1,0:T(8,128)(2,1)}, u32[]{:S(2)}, u32[]{:S(2)}) %all-to-all-start.3) | async-done | bytes 5505056 | tf_op jit(solution)/shard_map/all_to_all | solution.py:94
  522.0 3.6 reduce_sum.55
  525.6 2.5 copy.21
  528.1 4.2 gather_fusion.3
  533.8 1.8 multiply_reduce_fusion
  (49 shorter events, 15.4 us)
Async XLA Ops:
  0.6 166.5 %copy-start = (bf16[1,256,1792]{2,1,0:T(8,128)(2,1)S(1)}, bf16[1,256,1792]{2,1,0:T(8,128)(2,1)}, u32[]{:S(2)}) copy-start(bf16[1,256,1792]{2,1,0:T(8,128)(2,1)} %param.14) | copy-start | bytes 2752516
  16.0 6.4 %copy-start.2 = (bf16[128,3584]{1,0:T(8,128)(2,1)S(1)}, bf16[128,3584]{1,0:T(8,128)(2,1)}, u32[]{:S(2)}) copy-start(bf16[128,3584]{1,0:T(8,128)(2,1)} %param.15) | copy-start | bytes 2752516
  16.0 125.3 %all-to-all-start = ((bf16[16,96,1792]{2,1,0:T(8,128)(2,1)}), bf16[16,96,1792]{2,1,0:T(8,128)(2,1)}, u32[]{:S(2)}, u32[]{:S(2)}) async-start(bf16[16,96,1792]{2,1,0:T(8,128)(2,1)} %bitcast.108), calls=%async_computation | async-start | bytes 11010048 | tf_op jit(solution)/shard_map/all_to_all | solution.py:80
  23.5 2.5 copy-start.12
  145.5 6.7 %copy-start.10 = (bf16[1,1792,256]{2,1,0:T(8,128)(2,1)S(1)}, bf16[1,1792,256]{2,1,0:T(8,128)(2,1)}, u32[]{:S(2)}) copy-start(bf16[1,1792,256]{2,1,0:T(8,128)(2,1)} %param.13) | copy-start | bytes 2752516
  145.5 125.6 %all-to-all-start.2 = ((bf16[16,96,1792]{2,1,0:T(8,128)(2,1)}), bf16[16,96,1792]{2,1,0:T(8,128)(2,1)}, u32[]{:S(2)}, u32[]{:S(2)}) async-start(bf16[16,96,1792]{2,1,0:T(8,128)(2,1)} %bitcast.107), calls=%async_computation.2 | async-start | bytes 11010048 | tf_op jit(solution)/shard_map/all_to_all | solution.py:81
  152.2 4.3 copy-start.8
  161.0 3.5 collective-permute-start
  164.8 1.8 copy-start.3
  271.1 125.5 %all-to-all-start.1 = ((bf16[16,96,1792]{2,1,0:T(8,128)(2,1)}), bf16[16,96,1792]{2,1,0:T(8,128)(2,1)}, u32[]{:S(2)}, u32[]{:S(2)}) async-start(bf16[16,96,1792]{2,1,0:T(8,128)(2,1)} %bitcast.105), calls=%async_computation.1 | async-start | bytes 11010048 | tf_op jit(solution)/shard_map/all_to_all | solution.py:93
  277.7 6.7 %copy-start.4 = (f32[2,1536,256]{2,1,0:T(8,128)S(1)}, f32[2,1536,256]{2,1,0:T(8,128)}, u32[]{:S(2)}) copy-start(f32[2,1536,256]{2,1,0:T(8,128)} %copy-done.3) | copy-start | bytes 9437188
  282.1 2.4 collective-permute-start.1
  284.4 1.2 copy-start.9
  285.2 2.0 copy-start.6
  285.6 1.7 copy-start.11
  396.6 125.5 %all-to-all-start.3 = ((bf16[16,96,1792]{2,1,0:T(8,128)(2,1)}), bf16[16,96,1792]{2,1,0:T(8,128)(2,1)}, u32[]{:S(2)}, u32[]{:S(2)}) async-start(bf16[16,96,1792]{2,1,0:T(8,128)(2,1)} %bitcast.106), calls=%async_computation.3 | async-start | bytes 11010048 | tf_op jit(solution)/shard_map/all_to_all | solution.py:94
  403.1 5.2 copy-start.7
  532.3 1.5 copy-start.5
  533.8 3.0 copy-start.1
where the time goes:
time: 540 us; the launch traced here: 537 us
  waiting for transfers between devices  400 us (74%)
  local copies, waits for them, and re-layouts  54.4 us (10%)
  matrix products  37.9 us (7%)
  starting transfers between devices  26.6 us (5%)
  other arithmetic  16.3 us (3%)
    all_to_all x1, waiting for transfers between devices, on_device(): lax.all_to_all(shaped[0], 'expert', split_axis=0, concat_axis=0, tiled=True)  105 us
    all_to_all x1, waiting for transfers between devices, on_device(): lax.all_to_all(pack(by_expert_grad), 'expert', split_axis=0, concat_axis=...  100 us
    all_to_all x1, waiting for transfers between devices, on_device(): lax.all_to_all(pack(by_expert_x), 'expert', split_axis=0, concat_axis=0,...  97.2 us
    all_to_all x1, waiting for transfers between devices, on_device(): lax.all_to_all(shaped[1], 'expert', split_axis=0, concat_axis=0, tiled=True)  92 us
    scatter x4, local copies, waits for them, and re-layouts, on_device(): empty.at[target, :, slot_pos]  20.4 us
  transfers between devices with their start and end apart: 6, of which 6 were waited for; matrix products, arithmetic and copies ran while one was open for 14% of the time, Pallas kernels for 0%

commit v1 on v0

v1 whole, which is shorter than its diff:
```python
import jax
import jax.numpy as jnp
from jax import lax
from jax.sharding import PartitionSpec as P

BF16 = jnp.bfloat16
F32 = jnp.float32


def swap(value, mask):
    pairs = [(source, source ^ mask) for source in range(lax.axis_size("expert"))]
    return lax.ppermute(value, "expert", pairs)


def dot(a, b, ca, cb):
    return lax.dot_general(a, b, (((ca,), (cb,)), ((), ())), preferred_element_type=F32)


def on_device(tokens, gates, routes, counts, w_gate, w_up, w_down, cotangent):
    peers = lax.axis_size("expert")
    tok_rows, topk = routes.shape
    width = tokens.shape[1]
    half = width // 2
    quarter = w_gate.shape[2]
    experts = peers // 8
    capacity = max(2, 3 * tok_rows * topk // (2 * experts))
    flat_n = tok_rows * topk
    slots = experts * capacity
    me = lax.axis_index("expert")
    mine, core = me // 8, me % 2

    gate_up = jnp.concatenate([w_gate[0], w_up[0]], axis=1)
    down = w_down[0]
    gate_up_z = swap(gate_up, 4)
    down_z = swap(down, 4)

    valid = jnp.arange(tok_rows, dtype=jnp.int32) < counts[0]
    target = jnp.where(valid[:, None], routes, experts).reshape(flat_n)
    onehot = (target[:, None] == jnp.arange(experts, dtype=jnp.int32)[None, :]).astype(F32)
    earlier = (
        jnp.arange(flat_n)[:, None] > jnp.arange(flat_n)[None, :]
    ).astype(BF16)
    before = dot(earlier, onehot.astype(BF16), 1, 0)
    slot_pos = jnp.sum(before * onehot, axis=1).astype(jnp.int32)
    place = jnp.where(target < experts, (target ^ mine) * capacity + slot_pos, slots)
    put = (place[:, None] == jnp.arange(slots, dtype=jnp.int32)[None, :]).astype(BF16)
    gate_flat = gates.reshape(flat_n)
    if topk == 1:
        tok_flat, cot_flat = tokens, cotangent
    else:
        tok_flat = jnp.repeat(tokens, topk, axis=0)
        cot_flat = jnp.repeat(cotangent, topk, axis=0)
    cot_rows = cot_flat.astype(F32)
    scaled = (gate_flat[:, None] * cot_rows).astype(BF16)

    def own_first(rows):
        return jnp.where(
            core == 0, rows, jnp.concatenate([rows[:, half:], rows[:, :half]], axis=1)
        )

    packed_x = dot(put, own_first(tok_flat), 0, 0).astype(BF16)
    packed_s = dot(put, own_first(scaled), 0, 0).astype(BF16)

    def dispatch(packed):
        here = packed[:capacity]
        others = jnp.concatenate(
            [
                swap(packed[d * capacity : (d + 1) * capacity], 8 * d)
                for d in range(1, experts)
            ],
            axis=0,
        )
        return jnp.concatenate([here, others, swap(here, 2), swap(others, 2)], axis=0)

    rows = dispatch(packed_x)
    grads = dispatch(packed_s)

    gate_up_c, down_c = swap(gate_up, 1), swap(down, 1)
    gate_up_zc, down_zc = swap(gate_up_z, 1), swap(down_z, 1)
    w_in = jnp.concatenate(
        [
            jnp.concatenate([gate_up, gate_up_z], axis=1),
            jnp.concatenate([gate_up_c, gate_up_zc], axis=1),
        ],
        axis=0,
    )
    w_out = jnp.concatenate(
        [
            jnp.concatenate([down, down_c], axis=1),
            jnp.concatenate([down_z, down_zc], axis=1),
        ],
        axis=0,
    )

    pre = dot(rows, w_in, 1, 0)
    g = jnp.concatenate([pre[:, :quarter], pre[:, 2 * quarter : 3 * quarter]], axis=1)
    u = jnp.concatenate([pre[:, quarter : 2 * quarter], pre[:, 3 * quarter :]], axis=1)
    sg = jax.nn.sigmoid(g)
    act = (g * sg * u).astype(BF16)

    def give_back(part):
        ready = part[:slots] + swap(part[slots:].astype(BF16), 2).astype(F32)
        ready = ready.astype(BF16)
        return jnp.concatenate(
            [ready[:capacity]]
            + [
                swap(ready[d * capacity : (d + 1) * capacity], 8 * d)
                for d in range(1, experts)
            ],
            axis=0,
        )

    back_out = give_back(dot(act, w_out, 1, 0))
    d_act = dot(grads, w_out, 1, 1)
    d_gate = (d_act * u * sg * (1.0 + g * (1.0 - sg))).astype(BF16)
    d_up = (d_act * g * sg).astype(BF16)
    d_pre = jnp.concatenate(
        [d_gate[:, :quarter], d_up[:, :quarter], d_gate[:, quarter:], d_up[:, quarter:]], axis=1
    )
    back_dx = give_back(dot(d_pre, w_in, 1, 1))

    in_theirs = dot(rows[:, half:], d_pre, 0, 0).astype(BF16)
    out_theirs = dot(act, grads[:, half:], 0, 0).astype(BF16)
    in_mine = dot(rows[:, :half], d_pre, 0, 0) + swap(in_theirs, 1).astype(F32)
    out_mine = dot(act, grads[:, :half], 0, 0) + swap(out_theirs, 1).astype(F32)
    in_sum = in_mine[:, : 2 * quarter] + swap(
        in_mine[:, 2 * quarter :].astype(BF16), 4
    ).astype(F32)
    out_sum = out_mine[:quarter] + swap(out_mine[quarter:].astype(BF16), 4).astype(F32)
    grad_in = in_sum.astype(BF16)
    grad_wd = out_sum.astype(BF16)

    out_rows = own_first(dot(put, back_out, 1, 0))
    dx_rows = own_first(dot(put, back_dx, 1, 0))
    mixed = jnp.sum(
        (gate_flat[:, None] * out_rows).reshape(tok_rows, topk, width), axis=1
    ).astype(BF16)
    grad_tokens = jnp.sum(dx_rows.reshape(tok_rows, topk, width), axis=1).astype(BF16)
    grad_gates = jnp.sum(cot_rows * out_rows, axis=1).reshape(tok_rows, topk)
    return (
        mixed,
        grad_tokens,
        grad_gates,
        grad_in[:, :quarter][None],
        grad_in[:, quarter:][None],
        grad_wd[None],
    )


def solution(mesh):
    both, rows = ("groups", "expert"), P(("groups", "expert"), None)
    block = P(both, None, None)
    weight = P("expert", None, None)
    return jax.shard_map(
        on_device,
        mesh=mesh,
        in_specs=(rows, rows, rows, P(both), weight, weight, weight, rows),
        out_specs=(rows, rows, rows, block, block, block),
        check_vma=False,
    )
```

time: 540 us -> 282 us (0.52)
  waiting for transfers between devices: 400 us -> 181 us
  local copies, waits for them, and re-layouts: 54.4 us -> 3.69 us
  other arithmetic: 16.3 us -> 38.5 us
  matrix products: 37.9 us -> 30.7 us
    all_to_all x4 -> x0, waiting for transfers between devices: 395 us -> none  [the longest x1 105 us: on_device(): lax.all_to_all(shaped[0], 'expert', split_axis=0, concat_axis=0, tiled=True)]
    ppermute x2 -> x20, waiting for transfers between devices: 5.4 us -> 181 us  [swap(): return lax.ppermute(value, 'expert', pairs)]
    concatenate x1 -> x4, other arithmetic: 0.01 us -> 33.1 us  [the longest x1 29.8 us: on_device(): jnp.concatenate([jnp.concatenate([gate_up, gate_up_z], axis=1), jnp.conca...]
    all_to_all x4 -> x0, starting transfers between devices: 26.1 us -> none  [the longest x1 6.69 us: on_device(): lax.all_to_all(pack(by_expert_grad), 'expert', split_axis=0, concat_axis=...]
    ppermute x2 -> x20, starting transfers between devices: 0.43 us -> 23 us  [swap(): return lax.ppermute(value, 'expert', pairs)]
    scatter x4 -> x0, local copies, waits for them, and re-layouts: 20.4 us -> none  [on_device(): empty.at[target, :, slot_pos]]
    gather x4 -> x0, local copies, waits for them, and re-layouts: 12.6 us -> none  [the longest x1 4.19 us: on_device(): summed_dx[safe_target, :, slot_pos].reshape(flat_n, width)]
    reduce_sum x3 -> x0, other arithmetic: 7.32 us -> none  [the longest x2 7.15 us: unpack(): jnp.sum(returned.reshape(experts, 4, 2, capacity, half).astype(jnp.float3...]
  transfers between devices with their start and end apart: 6 -> 20, of which waited for: 6 -> 8; matrix products, arithmetic and copies ran while one was open for 14% -> 22% of each run, Pallas kernels for 0% -> 0%
where the time goes in v1:
time: 282 us; the launch traced here: 279 us
  waiting for transfers between devices  181 us (64%)
  other arithmetic  38.5 us (14%)
  matrix products  30.7 us (11%)
  starting transfers between devices  23 us (8%)
  local copies, waits for them, and re-layouts  3.69 us (1%)
    ppermute x20, waiting for transfers between devices, swap(): return lax.ppermute(value, 'expert', pairs)  181 us
    dot_general x13, matrix products, dot(): lax.dot_general(a, b, (((ca,), (cb,)), ((), ())), preferred_element_type=...  30.7 us
    concatenate x1, other arithmetic, on_device(): jnp.concatenate([jnp.concatenate([gate_up, gate_up_z], axis=1), jnp.conca...  29.8 us
    ppermute x20, starting transfers between devices, swap(): return lax.ppermute(value, 'expert', pairs)  23 us
  transfers between devices with their start and end apart: 20, of which 8 were waited for; matrix products, arithmetic and copies ran while one was open for 22% of the time, Pallas kernels for 0%

profile of v1, /device:TPU:8, one launch (start us, length us, event | category | flops | bytes accessed | tf_op | source)
XLA Modules:
  0.0 278.7 jit_solution(3715712198796690184)
XLA Ops:
  0.7 2.9 %pad_maximum_fusion.2 = bf16[1792,512]{1,0:T(8,128)(2,1)} fusion(bf16[1792,256]{1,0:T(8,128)(2,1)} %bitcast.27, bf16[1792,256]{1,0:T(8,128)(2,1)} %bitcast.29), kind=kLoop, calls=%fused_computation.26 | loop fusion | flops 3670016 | bytes 3670016 | tf_op jit(solution)/shard_map/concatenate | solution.py:32
  5.3 1.8 convolution_convert_fusion.1
  7.1 3.1 %collective-permute-start = (bf16[96,3584]{1,0:T(8,128)(2,1)S(1)}, bf16[96,3584]{1,0:T(8,128)(2,1)S(1)}, u32[]{:S(2)}, u32[]{:S(2)}) collective-permute-start(bf16[96,3584]{1,0:T(8,128)(2,1)S(1)} %get-tuple-element.26), channel_id=1, source_target_pairs={{0,8},{1,9},{2,10},{3,11},{4,12},{5,13},{6,14},{7,15},{8,0},{9,1},... | collective-permute-start | bytes 2064392 | tf_op jit(solution)/shard_map/ppermute | solution.py:12
  10.2 1.5 collective-permute-start.1
  11.7 1.6 collective-permute-start.7
  13.6 45.4 %collective-permute-done.3 = bf16[1792,512]{1,0:T(8,128)(2,1)} collective-permute-done((bf16[1792,512]{1,0:T(8,128)(2,1)}, bf16[1792,512]{1,0:T(8,128)(2,1)}, u32[]{:S(2)}, u32[]{:S(2)}) %collective-permute-start.3) | collective-permute-done | bytes 1835040 | tf_op jit(solution)/shard_map/ppermute | solution.py:12
  59.7 2.7 collective-permute-done
  62.3 1.5 collective-permute-start.2
  63.9 2.5 collective-permute-start.11
  66.4 12.6 %collective-permute-done.2 = bf16[96,3584]{1,0:T(8,128)(2,1)S(1)} collective-permute-done((bf16[96,3584]{1,0:T(8,128)(2,1)S(1)}, bf16[96,3584]{1,0:T(8,128)(2,1)S(1)}, u32[]{:S(2)}, u32[]{:S(2)}) %collective-permute-start.2) | collective-permute-done | bytes 688160 | tf_op jit(solution)/shard_map/ppermute | solution.py:12
  79.2 17.1 %collective-permute-done.11 = bf16[96,3584]{1,0:T(8,128)(2,1)S(1)} collective-permute-done((bf16[96,3584]{1,0:T(8,128)(2,1)S(1)}, bf16[96,3584]{1,0:T(8,128)(2,1)S(1)}, u32[]{:S(2)}, u32[]{:S(2)}) %collective-permute-start.11) | collective-permute-done | bytes 688160 | tf_op jit(solution)/shard_map/ppermute | solution.py:12
  96.3 1.5 collective-permute-start.12
  98.4 29.8 %maximum_maximum_fusion = bf16[3584,1024]{1,0:T(8,128)(2,1)S(1)} fusion(bf16[1792,512]{1,0:T(8,128)(2,1)S(1)} %collective-permute-done.5, bf16[1792,512]{1,0:T(8,128)(2,1)S(1)} %collective-permute-done.4, bf16[1792,512]{1,0:T(8,128)(2,1)} %collective-permute-done.3, bf16[1792,256]{1,0:T(8,128)(2,1)S(1)} %bitcast.28, bf16[1792,256]{1,0:T(8,128)(2,1)S(1)} %bitcast.30), kind=kLoop, calls=%fused_computation | loop fusion | flops 36700160 | bytes 14680064 | tf_op jit(solution)/shard_map/concatenate | solution.py:80
  128.2 3.0 %fusion.43 = f32[384,1024]{1,0:T(8,128)S(1)} fusion(bf16[3584,1024]{1,0:T(8,128)(2,1)S(1)} %maximum_maximum_fusion, bf16[96,3584]{1,0:T(8,128)(2,1)S(1)} %collective-permute-done.2, bf16[96,3584]{1,0:T(8,128)(2,1)S(1)} %collective-permute-done.1, bf16[96,3584]{1,0:T(8,128)(2,1)S(1)} %collective-permute-done, bf16[96,3584]{1,0:T(8,128)(2,1)S(1)} %get-tuple-element.25), kind=kOutput, calls=%fused_computation.86 | convolution fusion | flops 2829582336 | bytes 11665408 | tf_op jit(solution)/shard_map/dot_general | solution.py:16
  131.5 3.4 %multiply_convert_fusion.2 = (bf16[384,512]{1,0:T(8,128)(2,1)S(1)}, bf16[384,512]{1,0:T(8,128)(2,1)S(1)}, bf16[384,512]{1,0:T(8,128)(2,1)S(1)}) fusion(f32[384,256]{1,0:T(8,128)S(1)} %get-tuple-element.16, f32[384,256]{1,0:T(8,128)S(1)} %get-tuple-element.17, f32[384,256]{1,0:T(8,128)S(1)} %get-tuple-element.18, f32[384,256]{1,0:T(8,128)S(1)} %get-tuple-element.15, ...), kind=kOutput, calls=%fused_computation.60 | convolution fusion | flops 1438515200 | bytes 9175040 | tf_op jit(solution)/shard_map/dot_general | solution.py:16
  134.9 3.0 %fusion.42 = f32[384,3584]{1,0:T(8,128)S(1)} fusion(bf16[3584,1024]{1,0:T(8,128)(2,1)S(1)} %maximum_maximum_fusion, bf16[384,256]{1,0:T(8,128)(2,1)S(1)} %get-tuple-element.37, bf16[384,256]{1,0:T(8,128)(2,1)S(1)} %get-tuple-element.34, bf16[384,256]{1,0:T(8,128)(2,1)S(1)} %get-tuple-element.38, bf16[384,256]{1,0:T(8,128)(2,1)S(1)} %get-tuple-element.33), kind=kOutput, calls=%fused_computation.85 | convolution fusion | flops 2821718016 | bytes 13631488 | tf_op jit(solution)/shard_map/dot_general | solution.py:16
  138.1 1.6 collective-permute-start.14
  139.9 1.1 convolution_convert_fusion.3
  141.3 11.3 %fusion.28 = f32[384,3584]{1,0:T(8,128)S(1)} fusion(bf16[384,512]{1,0:T(8,128)(2,1)S(1)} %get-tuple-element.13, bf16[256,1792]{1,0:T(8,128)(2,1)} %collective-permute-done.8, bf16[256,1792]{1,0:T(8,128)(2,1)S(1)} %collective-permute-done.7, bf16[256,1792]{1,0:T(8,128)(2,1)S(1)} %copy-done.8, bf16[256,1792]{1,0:T(8,128)(2,1)S(1)} %bitcast.37), kind=kOutput, calls=%fused_computation.64 | convolution fusion | flops 1423966208 | bytes 9568256 | tf_op jit(solution)/shard_map/dot_general | solution.py:16
  153.4 2.1 convolution_convert_fusion.2
  155.6 15.6 %collective-permute-done.14 = bf16[192,3584]{1,0:T(8,128)(2,1)S(1)} collective-permute-done((bf16[192,3584]{1,0:T(8,128)(2,1)S(1)}, bf16[192,3584]{1,0:T(8,128)(2,1)S(1)}, u32[]{:S(2)}, u32[]{:S(2)}) %collective-permute-start.14) | collective-permute-done | bytes 1376288 | tf_op jit(solution)/shard_map/ppermute | solution.py:12
  171.5 3.4 %collective-permute-start.15 = (bf16[96,3584]{1,0:T(8,128)(2,1)S(1)}, bf16[96,3584]{1,0:T(8,128)(2,1)S(1)}, u32[]{:S(2)}, u32[]{:S(2)}) collective-permute-start(bf16[96,3584]{1,0:T(8,128)(2,1)S(1)} %get-tuple-element.20), channel_id=1, source_target_pairs={{0,8},{1,9},{2,10},{3,11},{4,12},{5,13},{6,14},{7,15},{8,0},{9,1},... | collective-permute-start | bytes 2064392 | tf_op jit(solution)/shard_map/ppermute | solution.py:12
  174.9 25.3 %collective-permute-done.9 = bf16[192,3584]{1,0:T(8,128)(2,1)S(1)} collective-permute-done((bf16[192,3584]{1,0:T(8,128)(2,1)S(1)}, bf16[192,3584]{1,0:T(8,128)(2,1)S(1)}, u32[]{:S(2)}, u32[]{:S(2)}) %collective-permute-start.9) | collective-permute-done | bytes 1376288 | tf_op jit(solution)/shard_map/ppermute | solution.py:12
  200.6 3.4 %collective-permute-start.10 = (bf16[96,3584]{1,0:T(8,128)(2,1)S(1)}, bf16[96,3584]{1,0:T(8,128)(2,1)S(1)}, u32[]{:S(2)}, u32[]{:S(2)}) collective-permute-start(bf16[96,3584]{1,0:T(8,128)(2,1)S(1)} %get-tuple-element.24), channel_id=1, source_target_pairs={{0,8},{1,9},{2,10},{3,11},{4,12},{5,13},{6,14},{7,15},{8,0},{9,1},... | collective-permute-start | bytes 2064392 | tf_op jit(solution)/shard_map/ppermute | solution.py:12
  204.0 1.1 convert_add_fusion.1
  205.8 25.7 %collective-permute-done.10 = bf16[96,3584]{1,0:T(8,128)(2,1)S(1)} collective-permute-done((bf16[96,3584]{1,0:T(8,128)(2,1)S(1)}, bf16[96,3584]{1,0:T(8,128)(2,1)S(1)}, u32[]{:S(2)}, u32[]{:S(2)}) %collective-permute-start.10) | collective-permute-done | bytes 688160 | tf_op jit(solution)/shard_map/ppermute | solution.py:12
  232.1 2.1 convert_add_fusion
  234.5 1.4 collective-permute-start.17
  236.0 1.8 fusion.4
  237.7 1.1 fusion.6
  240.0 36.8 %collective-permute-done.17 = bf16[1792,512]{1,0:T(8,128)(2,1)S(1)} collective-permute-done((bf16[1792,512]{1,0:T(8,128)(2,1)S(1)}, bf16[1792,512]{1,0:T(8,128)(2,1)S(1)}, u32[]{:S(2)}, u32[]{:S(2)}) %collective-permute-start.17) | collective-permute-done | bytes 1835040 | tf_op jit(solution)/shard_map/ppermute | solution.py:12
  277.4 1.3 slice_bitcast_fusion
  (67 shorter events, 8.5 us)
Async XLA Ops:
  0.6 3.6 %copy-start.5 = (s32[128,1]{0,1:T(1,128)S(1)}, s32[128,1]{0,1:T(1,128)}, u32[]{:S(2)}) copy-start(s32[128,1]{0,1:T(1,128)} %param.10) | copy-start | bytes 1540
  0.6 3.7 %copy-start.3 = (bf16[128,3584]{1,0:T(8,128)(2,1)S(1)}, bf16[128,3584]{1,0:T(8,128)(2,1)}, u32[]{:S(2)}) copy-start(bf16[128,3584]{1,0:T(8,128)(2,1)} %param.8) | copy-start | bytes 2752516
  3.5 94.8 %collective-permute-start.4 = (bf16[1792,512]{1,0:T(8,128)(2,1)}, bf16[1792,512]{1,0:T(8,128)(2,1)S(1)}, u32[]{:S(2)}, u32[]{:S(2)}) collective-permute-start(bf16[1792,512]{1,0:T(8,128)(2,1)} %pad_maximum_fusion.2), channel_id=1, source_target_pairs={{0,1},{1,0},{2,3},{3,2},{4,5},{5,4},{6,7},{7,6},{8,9},{9,8},{10,11... | collective-permute-start | bytes 5505032 | tf_op jit(solution)/shard_map/ppermute | solution.py:12
  3.5 55.5 %collective-permute-start.3 = (bf16[1792,512]{1,0:T(8,128)(2,1)}, bf16[1792,512]{1,0:T(8,128)(2,1)}, u32[]{:S(2)}, u32[]{:S(2)}) collective-permute-start(bf16[1792,512]{1,0:T(8,128)(2,1)} %pad_maximum_fusion.2), channel_id=1, source_target_pairs={{0,4},{1,5},{2,6},{3,7},{4,0},{5,1},{6,2},{7,3},{8,12},{9,13},{10,... | collective-permute-start | bytes 5505032 | tf_op jit(solution)/shard_map/ppermute | solution.py:12
  5.2 6.5 %copy-start.6 = (bf16[1,256,1792]{2,1,0:T(8,128)(2,1)S(1)}, bf16[1,256,1792]{2,1,0:T(8,128)(2,1)}, u32[]{:S(2)}) copy-start(bf16[1,256,1792]{2,1,0:T(8,128)(2,1)} %param.14) | copy-start | bytes 2752516
  5.2 8.1 %copy-start.2 = (bf16[128,3584]{1,0:T(8,128)(2,1)S(1)}, bf16[128,3584]{1,0:T(8,128)(2,1)}, u32[]{:S(2)}) copy-start(bf16[128,3584]{1,0:T(8,128)(2,1)} %param.15) | copy-start | bytes 2752516
  5.2 8.1 %copy-start.4 = (f32[128,1]{0,1:T(1,128)S(1)}, f32[128,1]{0,1:T(1,128)}, u32[]{:S(2)}) copy-start(f32[128,1]{0,1:T(1,128)} %param.9) | copy-start | bytes 1540
  7.1 55.2 %collective-permute-start = (bf16[96,3584]{1,0:T(8,128)(2,1)S(1)}, bf16[96,3584]{1,0:T(8,128)(2,1)S(1)}, u32[]{:S(2)}, u32[]{:S(2)}) collective-permute-start(bf16[96,3584]{1,0:T(8,128)(2,1)S(1)} %get-tuple-element.26), channel_id=1, source_target_pairs={{0,8},{1,9},{2,10},{3,11},{4,12},{5,13},{6,14},{7,15},{8,0},{9,1},... | collective-permute-start | bytes 2064392 | tf_op jit(solution)/shard_map/ppermute | solution.py:12
  10.2 53.7 %collective-permute-start.1 = (bf16[96,3584]{1,0:T(8,128)(2,1)S(1)}, bf16[96,3584]{1,0:T(8,128)(2,1)S(1)}, u32[]{:S(2)}, u32[]{:S(2)}) collective-permute-start(bf16[96,3584]{1,0:T(8,128)(2,1)S(1)} %get-tuple-element.25), channel_id=1, source_target_pairs={{0,2},{1,3},{2,0},{3,1},{4,6},{5,7},{6,4},{7,5},{8,10},{9,11},{10,... | collective-permute-start | bytes 2064392 | tf_op jit(solution)/shard_map/ppermute | solution.py:12
  11.7 86.1 %collective-permute-start.7 = (bf16[256,1792]{1,0:T(8,128)(2,1)S(1)}, bf16[256,1792]{1,0:T(8,128)(2,1)S(1)}, u32[]{:S(2)}, u32[]{:S(2)}) collective-permute-start(bf16[256,1792]{1,0:T(8,128)(2,1)S(1)} %bitcast.34), channel_id=1, source_target_pairs={{0,4},{1,5},{2,6},{3,7},{4,0},{5,1},{6,2},{7,3},{8,12},{9,13},{10,... | collective-permute-start | bytes 2752520 | tf_op jit(solution)/shard_map/ppermute | solution.py:12
  59.0 39.4 %collective-permute-start.5 = (bf16[1792,512]{1,0:T(8,128)(2,1)}, bf16[1792,512]{1,0:T(8,128)(2,1)S(1)}, u32[]{:S(2)}, u32[]{:S(2)}) collective-permute-start(bf16[1792,512]{1,0:T(8,128)(2,1)} %collective-permute-done.3), channel_id=1, source_target_pairs={{0,1},{1,0},{2,3},{3,2},{4,5},{5,4},{6,7},{7,6},{8,9},{9,8},{10,11... | collective-permute-start | bytes 5505032 | tf_op jit(solution)/shard_map/ppermute | solution.py:12
  62.3 16.7 %collective-permute-start.2 = (bf16[96,3584]{1,0:T(8,128)(2,1)S(1)}, bf16[96,3584]{1,0:T(8,128)(2,1)S(1)}, u32[]{:S(2)}, u32[]{:S(2)}) collective-permute-start(bf16[96,3584]{1,0:T(8,128)(2,1)S(1)} %collective-permute-done), channel_id=1, source_target_pairs={{0,2},{1,3},{2,0},{3,1},{4,6},{5,7},{6,4},{7,5},{8,10},{9,11},{10,... | collective-permute-start | bytes 2064392 | tf_op jit(solution)/shard_map/ppermute | solution.py:12
  63.9 34.5 %copy-start = (bf16[1,1792,256]{2,1,0:T(8,128)(2,1)S(1)}, bf16[1,1792,256]{2,1,0:T(8,128)(2,1)}, u32[]{:S(2)}) copy-start(bf16[1,1792,256]{2,1,0:T(8,128)(2,1)} %param.13) | copy-start | bytes 2752516
  63.9 34.5 %copy-start.1 = (bf16[1,1792,256]{2,1,0:T(8,128)(2,1)S(1)}, bf16[1,1792,256]{2,1,0:T(8,128)(2,1)}, u32[]{:S(2)}) copy-start(bf16[1,1792,256]{2,1,0:T(8,128)(2,1)} %param.12) | copy-start | bytes 2752516
  63.9 32.4 %collective-permute-start.11 = (bf16[96,3584]{1,0:T(8,128)(2,1)S(1)}, bf16[96,3584]{1,0:T(8,128)(2,1)S(1)}, u32[]{:S(2)}, u32[]{:S(2)}) collective-permute-start(bf16[96,3584]{1,0:T(8,128)(2,1)S(1)} %get-tuple-element.22), channel_id=1, source_target_pairs={{0,8},{1,9},{2,10},{3,11},{4,12},{5,13},{6,14},{7,15},{8,0},{9,1},... | collective-permute-start | bytes 2064392 | tf_op jit(solution)/shard_map/ppermute | solution.py:12
  79.0 52.4 %collective-permute-start.6 = (bf16[256,1792]{1,0:T(8,128)(2,1)S(1)}, bf16[256,1792]{1,0:T(8,128)(2,1)S(1)}, u32[]{:S(2)}, u32[]{:S(2)}) collective-permute-start(bf16[256,1792]{1,0:T(8,128)(2,1)S(1)} %bitcast.35), channel_id=1, source_target_pairs={{0,1},{1,0},{2,3},{3,2},{4,5},{5,4},{6,7},{7,6},{8,9},{9,8},{10,11... | collective-permute-start | bytes 2752520 | tf_op jit(solution)/shard_map/ppermute | solution.py:12
  96.3 35.1 %collective-permute-start.12 = (bf16[96,3584]{1,0:T(8,128)(2,1)S(1)}, bf16[96,3584]{1,0:T(8,128)(2,1)S(1)}, u32[]{:S(2)}, u32[]{:S(2)}) collective-permute-start(bf16[96,3584]{1,0:T(8,128)(2,1)S(1)} %get-tuple-element.21), channel_id=1, source_target_pairs={{0,2},{1,3},{2,0},{3,1},{4,6},{5,7},{6,4},{7,5},{8,10},{9,11},{10,... | collective-permute-start | bytes 2064392 | tf_op jit(solution)/shard_map/ppermute | solution.py:12
  97.8 33.6 %collective-permute-start.13 = (bf16[96,3584]{1,0:T(8,128)(2,1)S(1)}, bf16[96,3584]{1,0:T(8,128)(2,1)S(1)}, u32[]{:S(2)}, u32[]{:S(2)}) collective-permute-start(bf16[96,3584]{1,0:T(8,128)(2,1)S(1)} %collective-permute-done.11), channel_id=1, source_target_pairs={{0,2},{1,3},{2,0},{3,1},{4,6},{5,7},{6,4},{7,5},{8,10},{9,11},{10,... | collective-permute-start | bytes 2064392 | tf_op jit(solution)/shard_map/ppermute | solution.py:12
  98.4 33.1 %collective-permute-start.8 = (bf16[256,1792]{1,0:T(8,128)(2,1)S(1)}, bf16[256,1792]{1,0:T(8,128)(2,1)}, u32[]{:S(2)}, u32[]{:S(2)}) collective-permute-start(bf16[256,1792]{1,0:T(8,128)(2,1)S(1)} %collective-permute-done.7), channel_id=1, source_target_pairs={{0,1},{1,0},{2,3},{3,2},{4,5},{5,4},{6,7},{7,6},{8,9},{9,8},{10,11... | collective-permute-start | bytes 2752520 | tf_op jit(solution)/shard_map/ppermute | solution.py:12
  131.4 3.4 %copy-start.7 = (bf16[256,1792]{1,0:T(8,128)(2,1)}, bf16[256,1792]{1,0:T(8,128)(2,1)S(1)}, u32[]{:S(2)}) copy-start(bf16[256,1792]{1,0:T(8,128)(2,1)S(1)} %collective-permute-done.6) | copy-start | bytes 2752516
  138.1 33.0 %collective-permute-start.14 = (bf16[192,3584]{1,0:T(8,128)(2,1)S(1)}, bf16[192,3584]{1,0:T(8,128)(2,1)S(1)}, u32[]{:S(2)}, u32[]{:S(2)}) collective-permute-start(bf16[192,3584]{1,0:T(8,128)(2,1)S(1)} %slice.221), channel_id=1, source_target_pairs={{0,2},{1,3},{2,0},{3,1},{4,6},{5,7},{6,4},{7,5},{8,10},{9,11},{10,... | collective-permute-start | bytes 4128776 | tf_op jit(solution)/shard_map/ppermute | solution.py:12
  139.9 1.4 copy-start.8
  141.0 63.0 %collective-permute-start.18 = (bf16[512,1792]{1,0:T(8,128)(2,1)S(1)}, bf16[512,1792]{1,0:T(8,128)(2,1)S(1)}, u32[]{:S(2)}, u32[]{:S(2)}) collective-permute-start(bf16[512,1792]{1,0:T(8,128)(2,1)S(1)} %convolution_convert_fusion.3), channel_id=1, source_target_pairs={{0,1},{1,0},{2,3},{3,2},{4,5},{5,4},{6,7},{7,6},{8,9},{9,8},{10,11... | collective-permute-start | bytes 5505032 | tf_op jit(solution)/shard_map/ppermute | solution.py:12
  152.8 47.4 %collective-permute-start.9 = (bf16[192,3584]{1,0:T(8,128)(2,1)S(1)}, bf16[192,3584]{1,0:T(8,128)(2,1)S(1)}, u32[]{:S(2)}, u32[]{:S(2)}) collective-permute-start(bf16[192,3584]{1,0:T(8,128)(2,1)S(1)} %slice.222), channel_id=1, source_target_pairs={{0,2},{1,3},{2,0},{3,1},{4,6},{5,7},{6,4},{7,5},{8,10},{9,11},{10,... | collective-permute-start | bytes 4128776 | tf_op jit(solution)/shard_map/ppermute | solution.py:12
  155.5 76.6 %collective-permute-start.16 = (bf16[1792,1024]{1,0:T(8,128)(2,1)S(1)}, bf16[1792,1024]{1,0:T(8,128)(2,1)S(1)}, u32[]{:S(2)}, u32[]{:S(2)}) collective-permute-start(bf16[1792,1024]{1,0:T(8,128)(2,1)S(1)} %convolution_convert_fusion.2), channel_id=1, source_target_pairs={{0,1},{1,0},{2,3},{3,2},{4,5},{5,4},{6,7},{7,6},{8,9},{9,8},{10,11... | collective-permute-start | bytes 11010056 | tf_op jit(solution)/shard_map/ppermute | solution.py:12
  171.5 33.8 %collective-permute-start.15 = (bf16[96,3584]{1,0:T(8,128)(2,1)S(1)}, bf16[96,3584]{1,0:T(8,128)(2,1)S(1)}, u32[]{:S(2)}, u32[]{:S(2)}) collective-permute-start(bf16[96,3584]{1,0:T(8,128)(2,1)S(1)} %get-tuple-element.20), channel_id=1, source_target_pairs={{0,8},{1,9},{2,10},{3,11},{4,12},{5,13},{6,14},{7,15},{8,0},{9,1},... | collective-permute-start | bytes 2064392 | tf_op jit(solution)/shard_map/ppermute | solution.py:12
  200.6 30.9 %collective-permute-start.10 = (bf16[96,3584]{1,0:T(8,128)(2,1)S(1)}, bf16[96,3584]{1,0:T(8,128)(2,1)S(1)}, u32[]{:S(2)}, u32[]{:S(2)}) collective-permute-start(bf16[96,3584]{1,0:T(8,128)(2,1)S(1)} %get-tuple-element.24), channel_id=1, source_target_pairs={{0,8},{1,9},{2,10},{3,11},{4,12},{5,13},{6,14},{7,15},{8,0},{9,1},... | collective-permute-start | bytes 2064392 | tf_op jit(solution)/shard_map/ppermute | solution.py:12
  205.2 33.6 %collective-permute-start.19 = (bf16[256,1792]{1,0:T(8,128)(2,1)S(1)}, bf16[256,1792]{1,0:T(8,128)(2,1)S(1)}, u32[]{:S(2)}, u32[]{:S(2)}) collective-permute-start(bf16[256,1792]{1,0:T(8,128)(2,1)S(1)} %slice.223), channel_id=1, source_target_pairs={{0,4},{1,5},{2,6},{3,7},{4,0},{5,1},{6,2},{7,3},{8,12},{9,13},{10,... | collective-permute-start | bytes 2752520 | tf_op jit(solution)/shard_map/ppermute | solution.py:12
  234.5 42.3 %collective-permute-start.17 = (bf16[1792,512]{1,0:T(8,128)(2,1)S(1)}, bf16[1792,512]{1,0:T(8,128)(2,1)S(1)}, u32[]{:S(2)}, u32[]{:S(2)}) collective-permute-start(bf16[1792,512]{1,0:T(8,128)(2,1)S(1)} %slice.220), channel_id=1, source_target_pairs={{0,4},{1,5},{2,6},{3,7},{4,0},{5,1},{6,2},{7,3},{8,12},{9,13},{10,... | collective-permute-start | bytes 5505032 | tf_op jit(solution)/shard_map/ppermute | solution.py:12

commit v2 on v1

v2 whole, which is shorter than its diff:
```python
import functools

import jax
import jax.numpy as jnp
from jax import lax
from jax.experimental import pallas as pl
from jax.experimental.pallas import tpu as pltpu
from jax.sharding import PartitionSpec as P

BF16 = jnp.bfloat16
F32 = jnp.float32


def swap(value, mask):
    pairs = [(source, source ^ mask) for source in range(lax.axis_size("expert"))]
    return lax.ppermute(value, "expert", pairs)


def dot(a, b, ca, cb):
    return lax.dot_general(a, b, (((ca,), (cb,)), ((), ())), preferred_element_type=F32)


def layer_kernel(
    cap, half, quarter,
    px, ps, wg, wu, wd,
    bo, bx, og, ou, od,
    rows, grads, gates_w, ups_w, downs_w, g_buf, u_buf, act, dd,
    out_keep, out_send, out_recv, dx_keep, dx_send, dx_recv,
    tg, tu, td, rg, ru, rd, zsg, zsu, zsd, zrg, zru, zrd,
    send_sem, recv_sem, local_sem,
):
    me, group = lax.axis_index("expert"), lax.axis_index("groups")
    slots = 2 * cap
    step = cap // 2

    def partner(mask):
        return me + mask - 2 * mask * lax.rem(me // mask, 2)

    core, near, far, home = (
        {"expert": partner(1)}, {"expert": partner(2)}, {"expert": partner(4)},
        {"expert": partner(8)},
    )
    twin = {"groups": 1 - group}
    barrier = pltpu.get_barrier_semaphore()
    for other in (core, near, far, home, twin):
        pl.semaphore_signal(barrier, inc=1, device_id=other, device_id_type=pl.DeviceIdType.MESH)
    pl.semaphore_wait(barrier, 5)

    sent = []

    def send(src, dst, to):
        number = len(sent)
        copy = pltpu.make_async_remote_copy(
            src_ref=src, dst_ref=dst, send_sem=send_sem.at[number],
            recv_sem=recv_sem.at[number], device_id=to,
            device_id_type=pl.DeviceIdType.MESH,
        )
        copy.start()
        sent.append(copy)
        return copy

    locals_ = []

    def local(src, dst):
        copy = pltpu.make_async_copy(src, dst, local_sem.at[len(locals_)])
        copy.start()
        locals_.append(copy)
        return copy

    def part(ref, start, size):
        return ref.at[pl.ds(start, size)]

    over_x = [
        send(part(px, cap + i * step, step), part(rows, cap + i * step, step), home)
        for i in range(2)
    ]
    over_s = [
        send(part(ps, cap + i * step, step), part(grads, cap + i * step, step), home)
        for i in range(2)
    ]
    near_x = [send(part(px, 0, cap), part(rows, slots, cap), near)]
    near_s = [send(part(ps, 0, cap), part(grads, slots, cap), near)]
    weights = ((wg, gates_w), (wu, ups_w), (wd, downs_w))

    def group_half(ref, which):
        size = ref.shape[0] // 2
        return ref.at[pl.ds(pl.multiple_of(which * size, size), size)]

    far_w = [send(group_half(w, group), group_half(b.at[2], group), far) for w, b in weights]
    core_w = [send(w, b.at[1], core) for w, b in weights]
    own_w = [local(w, b.at[0]) for w, b in weights]
    own_r = [local(part(px, 0, cap), part(rows, 0, cap)),
             local(part(ps, 0, cap), part(grads, 0, cap))]

    for i in range(2):
        over_x[i].wait_recv()
        block = part(rows, cap + i * step, step)
        near_x.append(send(block, part(rows, slots + cap + i * step, step), near))
    twin_w = []
    for i, (w, b) in enumerate(weights):
        far_w[i].wait_recv()
        twin_w.append(send(group_half(b.at[2], group), group_half(b.at[2], group), twin))
    far_core_w = []
    for i, (w, b) in enumerate(weights):
        twin_w[i].wait_recv()
        far_core_w.append(send(b.at[2], b.at[3], core))
    for i in range(2):
        over_s[i].wait_recv()
        block = part(grads, cap + i * step, step)
        near_s.append(send(block, part(grads, slots + cap + i * step, step), near))

    for copy in own_w + own_r:
        copy.wait()
    for copy in near_x + core_w + far_core_w:
        copy.wait_recv()

    for q in range(2):
        columns = slice(q * quarter, (q + 1) * quarter)
        left, right = rows[:, :half], rows[:, half:]
        g = dot(left, gates_w[2 * q], 1, 0) + dot(right, gates_w[2 * q + 1], 1, 0)
        u = dot(left, ups_w[2 * q], 1, 0) + dot(right, ups_w[2 * q + 1], 1, 0)
        g_buf[:, columns] = g
        u_buf[:, columns] = u
        act[:, columns] = (g * jax.nn.sigmoid(g) * u).astype(BF16)

    tile = half // 2

    def give(keep, away, arrived, make):
        for h in range(2):
            @pl.loop(0, 2)
            def _(t):
                at = pl.multiple_of(t * tile, tile)
                value = make(h, pl.ds(at, tile)).astype(BF16)
                columns = pl.ds(pl.multiple_of(h * half + t * tile, tile), tile)
                keep[:, columns] = value[:slots]
                away[:, columns] = value[slots:]
        return [
            send(part(away, at, step), part(arrived, at, step), near)
            for at in (cap, cap + step, 0, step)
        ]

    def make_out(h, columns):
        return dot(act[:, :quarter], downs_w[h, :, columns], 1, 0) + dot(
            act[:, quarter:], downs_w[2 + h, :, columns], 1, 0
        )

    near_out = give(out_keep, out_send, out_recv, make_out)

    for copy in near_s:
        copy.wait_recv()
    for q in range(2):
        columns = slice(q * quarter, (q + 1) * quarter)
        d_act = dot(grads[:, :half], downs_w[2 * q], 1, 1) + dot(
            grads[:, half:], downs_w[2 * q + 1], 1, 1
        )
        g, u = g_buf[:, columns], u_buf[:, columns]
        sg = jax.nn.sigmoid(g)
        dd[:, columns] = (d_act * u * sg * (1.0 + g * (1.0 - sg))).astype(BF16)
        dd[:, slice((2 + q) * quarter, (3 + q) * quarter)] = (d_act * g * sg).astype(BF16)

    @pl.loop(0, 2)
    def _(t):
        at = pl.multiple_of(t * tile, tile)
        value = dot(act[...], grads[:, pl.ds(pl.multiple_of(half + at, tile), tile)], 0, 0)
        value = value.astype(BF16)
        td[0, :, pl.ds(at, tile)] = value[:quarter]
        td[1, :, pl.ds(at, tile)] = value[quarter:]

    core_d = [send(td.at[q], rd.at[q], core) for q in (1, 0)]
    width_step = 256

    @pl.loop(0, half // width_step)
    def _(t):
        at = pl.multiple_of(t * width_step, width_step)
        value = dot(rows[:, pl.ds(pl.multiple_of(half + at, width_step), width_step)], dd[...], 0, 0)
        value = value.astype(BF16)
        for q in range(2):
            tg[q, pl.ds(at, width_step)] = value[:, q * quarter : (q + 1) * quarter]
            tu[q, pl.ds(at, width_step)] = value[:, (2 + q) * quarter : (3 + q) * quarter]

    core_g = [send(tg.at[q], rg.at[q], core) for q in (1, 0)]
    core_u = [send(tu.at[q], ru.at[q], core) for q in (1, 0)]

    for copy in core_d:
        copy.wait_recv()

    @pl.loop(0, 2)
    def _(t):
        at = pl.multiple_of(t * tile, tile)
        value = dot(act[...], grads[:, pl.ds(at, tile)], 0, 0)
        od[:, pl.ds(at, tile)] = (value[:quarter] + rd[0, :, pl.ds(at, tile)].astype(F32)).astype(BF16)
        zsd[:, pl.ds(at, tile)] = (value[quarter:] + rd[1, :, pl.ds(at, tile)].astype(F32)).astype(BF16)

    far_d = send(zsd, zrd, far)

    for copy in core_g + core_u:
        copy.wait_recv()

    @pl.loop(0, half // width_step)
    def _(t):
        at = pl.ds(pl.multiple_of(t * width_step, width_step), width_step)
        value = dot(rows[:, at], dd[...], 0, 0)
        for column, got, mine, away in ((0, rg, og, zsg), (2, ru, ou, zsu)):
            first = value[:, column * quarter : (column + 1) * quarter]
            second = value[:, (column + 1) * quarter : (column + 2) * quarter]
            mine[at] = (first + got[0, at].astype(F32)).astype(BF16)
            away[at] = (second + got[1, at].astype(F32)).astype(BF16)

    far_g = send(zsg, zrg, far)
    far_u = send(zsu, zru, far)

    def make_dx(h, columns):
        value = dot(dd[:, :quarter], gates_w[h, columns], 1, 1)
        value = value + dot(dd[:, quarter : 2 * quarter], gates_w[2 + h, columns], 1, 1)
        value = value + dot(dd[:, 2 * quarter : 3 * quarter], ups_w[h, columns], 1, 1)
        return value + dot(dd[:, 3 * quarter :], ups_w[2 + h, columns], 1, 1)

    near_dx = give(dx_keep, dx_send, dx_recv, make_dx)

    homeward = []
    for keep, arrived, copies, result in (
        (out_keep, out_recv, near_out, bo), (dx_keep, dx_recv, near_dx, bx),
    ):
        for copy, at in zip(copies, (cap, cap + step, 0, step)):
            copy.wait_recv()
            total = keep[at : at + step].astype(F32) + arrived[at : at + step].astype(F32)
            keep[at : at + step] = total.astype(BF16)
            if at >= cap:
                homeward.append(send(part(keep, at, step), part(result, at, step), home))
            else:
                local(part(keep, at, step), part(result, at, step))

    for copy, mine, got in ((far_d, od, zrd), (far_g, og, zrg), (far_u, ou, zru)):
        copy.wait_recv()
        mine[...] = (mine[...].astype(F32) + got[...].astype(F32)).astype(BF16)
    for copy in homeward:
        copy.wait_recv()
    for copy in locals_[len(own_w + own_r):]:
        copy.wait()
    for copy in sent:
        copy.wait_send()


def layer(cap, packed_x, packed_s, wg, wu, wd):
    half, quarter = wg.shape
    slots = 2 * cap
    width = 2 * half
    count = 2 * slots
    vmem = lambda *shape, dtype=BF16: pltpu.VMEM(shape, dtype)
    back = jax.ShapeDtypeStruct((slots, width), BF16)
    like = lambda w: jax.ShapeDtypeStruct(w.shape, BF16)
    anywhere = pl.BlockSpec(memory_space=pl.ANY)
    inside = pl.BlockSpec(memory_space=pltpu.VMEM)
    ff = 2 * quarter
    copies = 43
    return pl.pallas_call(
        functools.partial(layer_kernel, cap, half, quarter),
        out_shape=(back, back, like(wg), like(wu), like(wd)),
        in_specs=[anywhere] * 5,
        out_specs=(anywhere, anywhere, inside, inside, inside),
        scratch_shapes=[
            vmem(count, width), vmem(count, width),
            vmem(4, half, quarter), vmem(4, half, quarter), vmem(4, quarter, half),
            vmem(count, ff, dtype=F32), vmem(count, ff, dtype=F32),
            vmem(count, ff), vmem(count, 2 * ff),
        ]
        + [vmem(slots, width)] * 6
        + [vmem(2, half, quarter), vmem(2, half, quarter), vmem(2, quarter, half)] * 2
        + [vmem(half, quarter), vmem(half, quarter), vmem(quarter, half)] * 2
        + [
            pltpu.SemaphoreType.DMA((copies,)),
            pltpu.SemaphoreType.DMA((copies,)),
            pltpu.SemaphoreType.DMA((16,)),
        ],
        compiler_params=pltpu.CompilerParams(
            collective_id=0, has_side_effects=True, vmem_limit_bytes=60 * 1024 * 1024
        ),
        cost_estimate=pl.CostEstimate(
            flops=18 * count * width * ff, bytes_accessed=40 * half * quarter * 2,
            transcendentals=2 * count * ff,
        ),
    )(packed_x, packed_s, wg, wu, wd)


def layer_by_permutes(experts, capacity, packed_x, packed_s, w_gate, w_up, w_down):
    half, quarter = w_gate.shape
    slots = experts * capacity
    gate_up = jnp.concatenate([w_gate, w_up], axis=1)
    down = w_down
    gate_up_z = swap(gate_up, 4)
    down_z = swap(down, 4)

    def dispatch(packed):
        here = packed[:capacity]
        others = jnp.concatenate(
            [
                swap(packed[d * capacity : (d + 1) * capacity], 8 * d)
                for d in range(1, experts)
            ],
            axis=0,
        )
        return jnp.concatenate([here, others, swap(here, 2), swap(others, 2)], axis=0)

    rows = dispatch(packed_x)
    grads = dispatch(packed_s)

    gate_up_c, down_c = swap(gate_up, 1), swap(down, 1)
    gate_up_zc, down_zc = swap(gate_up_z, 1), swap(down_z, 1)
    w_in = jnp.concatenate(
        [
            jnp.concatenate([gate_up, gate_up_z], axis=1),
            jnp.concatenate([gate_up_c, gate_up_zc], axis=1),
        ],
        axis=0,
    )
    w_out = jnp.concatenate(
        [
            jnp.concatenate([down, down_c], axis=1),
            jnp.concatenate([down_z, down_zc], axis=1),
        ],
        axis=0,
    )

    pre = dot(rows, w_in, 1, 0)
    g = jnp.concatenate([pre[:, :quarter], pre[:, 2 * quarter : 3 * quarter]], axis=1)
    u = jnp.concatenate([pre[:, quarter : 2 * quarter], pre[:, 3 * quarter :]], axis=1)
    sg = jax.nn.sigmoid(g)
    act = (g * sg * u).astype(BF16)

    def give_back(part):
        ready = part[:slots] + swap(part[slots:].astype(BF16), 2).astype(F32)
        ready = ready.astype(BF16)
        return jnp.concatenate(
            [ready[:capacity]]
            + [
                swap(ready[d * capacity : (d + 1) * capacity], 8 * d)
                for d in range(1, experts)
            ],
            axis=0,
        )

    back_out = give_back(dot(act, w_out, 1, 0))
    d_act = dot(grads, w_out, 1, 1)
    d_gate = (d_act * u * sg * (1.0 + g * (1.0 - sg))).astype(BF16)
    d_up = (d_act * g * sg).astype(BF16)
    d_pre = jnp.concatenate(
        [d_gate[:, :quarter], d_up[:, :quarter], d_gate[:, quarter:], d_up[:, quarter:]], axis=1
    )
    back_dx = give_back(dot(d_pre, w_in, 1, 1))

    in_theirs = dot(rows[:, half:], d_pre, 0, 0).astype(BF16)
    out_theirs = dot(act, grads[:, half:], 0, 0).astype(BF16)
    in_mine = dot(rows[:, :half], d_pre, 0, 0) + swap(in_theirs, 1).astype(F32)
    out_mine = dot(act, grads[:, :half], 0, 0) + swap(out_theirs, 1).astype(F32)
    in_sum = in_mine[:, : 2 * quarter] + swap(
        in_mine[:, 2 * quarter :].astype(BF16), 4
    ).astype(F32)
    out_sum = out_mine[:quarter] + swap(out_mine[quarter:].astype(BF16), 4).astype(F32)
    grad_in = in_sum.astype(BF16)
    return back_out, back_dx, grad_in[:, :quarter], grad_in[:, quarter:], out_sum.astype(BF16)


def on_device(tokens, gates, routes, counts, w_gate, w_up, w_down, cotangent):
    peers = lax.axis_size("expert")
    tok_rows, topk = routes.shape
    width = tokens.shape[1]
    half = width // 2
    experts = peers // 8
    capacity = max(2, 3 * tok_rows * topk // (2 * experts))
    flat_n = tok_rows * topk
    slots = experts * capacity
    me = lax.axis_index("expert")
    mine, core = me // 8, me % 2

    valid = jnp.arange(tok_rows, dtype=jnp.int32) < counts[0]
    target = jnp.where(valid[:, None], routes, experts).reshape(flat_n)
    onehot = (target[:, None] == jnp.arange(experts, dtype=jnp.int32)[None, :]).astype(F32)
    earlier = (
        jnp.arange(flat_n)[:, None] > jnp.arange(flat_n)[None, :]
    ).astype(BF16)
    before = dot(earlier, onehot.astype(BF16), 1, 0)
    slot_pos = jnp.sum(before * onehot, axis=1).astype(jnp.int32)
    place = jnp.where(target < experts, (target ^ mine) * capacity + slot_pos, slots)
    put = (place[:, None] == jnp.arange(slots, dtype=jnp.int32)[None, :]).astype(BF16)
    gate_flat = gates.reshape(flat_n)
    if topk == 1:
        tok_flat, cot_flat = tokens, cotangent
    else:
        tok_flat = jnp.repeat(tokens, topk, axis=0)
        cot_flat = jnp.repeat(cotangent, topk, axis=0)
    cot_rows = cot_flat.astype(F32)
    scaled = (gate_flat[:, None] * cot_rows).astype(BF16)

    def own_first(rows):
        return jnp.where(
            core == 0, rows, jnp.concatenate([rows[:, half:], rows[:, :half]], axis=1)
        )

    packed_x = dot(put, own_first(tok_flat), 0, 0).astype(BF16)
    packed_s = dot(put, own_first(scaled), 0, 0).astype(BF16)

    if experts == 2 and capacity % 32 == 0 and half % 256 == 0 and lax.axis_size("groups") == 2:
        back_out, back_dx, grad_wg, grad_wu, grad_wd = layer(
            capacity, packed_x, packed_s, w_gate[0], w_up[0], w_down[0]
        )
    else:
        back_out, back_dx, grad_wg, grad_wu, grad_wd = layer_by_permutes(
            experts, capacity, packed_x, packed_s, w_gate[0], w_up[0], w_down[0]
        )

    out_rows = own_first(dot(put, back_out, 1, 0))
    dx_rows = own_first(dot(put, back_dx, 1, 0))
    mixed = jnp.sum(
        (gate_flat[:, None] * out_rows).reshape(tok_rows, topk, width), axis=1
    ).astype(BF16)
    grad_tokens = jnp.sum(dx_rows.reshape(tok_rows, topk, width), axis=1).astype(BF16)
    grad_gates = jnp.sum(cot_rows * out_rows, axis=1).reshape(tok_rows, topk)
    return (
        mixed,
        grad_tokens,
        grad_gates,
        grad_wg[None],
        grad_wu[None],
        grad_wd[None],
    )


def solution(mesh):
    both, rows = ("groups", "expert"), P(("groups", "expert"), None)
    block = P(both, None, None)
    weight = P("expert", None, None)
    return jax.shard_map(
        on_device,
        mesh=mesh,
        in_specs=(rows, rows, rows, P(both), weight, weight, weight, rows),
        out_specs=(rows, rows, rows, block, block, block),
        check_vma=False,
    )
```

time: 282 us -> 218 us (0.77); the launches traced: 279 us -> 218 us
  Pallas kernels: 0 us -> 200 us
  waiting for transfers between devices: 181 us -> 0 us
  other arithmetic: 38.5 us -> 5.65 us
  matrix products: 30.7 us -> 5.99 us
  starting transfers between devices: 23 us -> 0 us
    pallas_call x0 -> x1, Pallas kernels: none -> 200 us  [layer(): pl.pallas_call(functools.partial(layer_kernel, cap, half, quarter), out_s...]
    ppermute x20 -> x0, waiting for transfers between devices: 181 us -> none  [swap(): return lax.ppermute(value, 'expert', pairs)]
    concatenate x4 -> x0, other arithmetic: 33.1 us -> none  [the longest x1 29.8 us: on_device(): jnp.concatenate([jnp.concatenate([gate_up, gate_up_z], axis=1), jnp.conca...]
    dot_general x13 -> x5, matrix products: 30.7 us -> 5.99 us  [dot(): lax.dot_general(a, b, (((ca,), (cb,)), ((), ())), preferred_element_type=...]
    ppermute x20 -> x0, starting transfers between devices: 23 us -> none  [swap(): return lax.ppermute(value, 'expert', pairs)]
    unnamed x18 -> x17, local copies, waits for them, and re-layouts: 0.05 us -> 4.42 us
  transfers between devices with their start and end apart: 20 -> 0, of which waited for: 8 -> 0; matrix products, arithmetic and copies ran while one was open for 22% -> 0% of each run, Pallas kernels for 0% -> 0%
where the time goes in v2:
time: 218 us
  Pallas kernels  200 us (92%)
  matrix products  5.99 us (3%)
  other arithmetic  5.65 us (3%)
  local copies, waits for them, and re-layouts  4.73 us (2%)
    pallas_call x1, Pallas kernels, layer(): pl.pallas_call(functools.partial(layer_kernel, cap, half, quarter), out_s...  200 us
    dot_general x5, matrix products, dot(): lax.dot_general(a, b, (((ca,), (cb,)), ((), ())), preferred_element_type=...  5.99 us
    unnamed x17, local copies, waits for them, and re-layouts  4.42 us

profile of v2, /device:TPU:8, one launch (start us, length us, event | category | flops | bytes accessed | tf_op | source)
XLA Modules:
  0.0 218.1 jit_solution(85192492561128504)
XLA Ops:
  1.3 0.7 fusion.20
  2.0 0.1 fusion.3
  2.1 0.7 fusion.16
  2.8 1.4 fusion
  4.2 0.1 fusion.23
  4.3 0.0 copy-start.1
  4.3 1.7 convolution_convert_fusion.ps
  6.0 0.0 copy-done.1
  6.0 0.1 fusion.24
  6.1 1.8 convolution_convert_fusion.1.px
  7.8 200.3 %shard_map.127 = (bf16[192,3584]{1,0:T(8,128)(2,1)}, bf16[192,3584]{1,0:T(8,128)(2,1)}, bf16[1792,256]{1,0:T(8,128)(2,1)}, bf16[1792,256]{1,0:T(8,128)(2,1)}, bf16[256,1792]{1,0:T(8,128)(2,1)}) custom-call(bf16[192,3584]{1,0:T(8,128)(2,1)} %convolution_convert_fusion.1.px, bf16[192,3584]{1,0:T(8,128)(2,1)} %convolution_convert_fusion.ps, ...), custom_call_target="tpu_custom_call" | custom-call | flops 12683575296 | bytes 36700160 | tf_op jit(solution)/shard_map/pallas_call | solution.py:256
  208.2 0.0 copy-start.2
  208.2 1.9 fusion.11
  210.1 0.0 copy-done.2
  210.1 0.5 fusion.10
  210.6 0.1 fusion.22
  210.6 1.1 fusion.2
  211.8 0.0 copy-start
  211.8 0.0 copy-start.6
  211.8 0.1 fusion.21
  211.9 1.1 copy-done
  213.0 0.0 copy-done.6
  213.0 0.0 copy-start.5
  213.0 1.8 fusion.1
  214.7 0.0 copy-start.4
  214.7 0.0 copy-done.5
  214.7 0.0 copy-start.3
  214.7 0.9 copy.18
  215.7 0.6 copy-done.4
  216.2 0.9 copy.19
  217.2 0.0 copy-done.3
  217.2 0.9 copy.20
Async XLA Ops:
  4.3 1.7 copy-start.1
  208.2 1.9 copy-start.2
  211.8 1.2 copy-start
  211.8 1.2 copy-start.6
  213.0 1.8 copy-start.5
  214.7 1.5 copy-start.4
  214.7 2.4 %copy-start.3 = (bf16[256,1792]{1,0:T(8,128)(2,1)S(1)}, bf16[256,1792]{1,0:T(8,128)(2,1)}, u32[]{:S(2)}) copy-start(bf16[256,1792]{1,0:T(8,128)(2,1)} %get-tuple-element.15) | copy-start | bytes 2752516

commit v3 on v2

--- a/solution.py
+++ b/solution.py
@@ -100,21 +100,13 @@
     for i, (w, b) in enumerate(weights):
         far_w[i].wait_recv()
         twin_w.append(send(group_half(b.at[2], group), group_half(b.at[2], group), twin))
-    far_core_w = []
-    for i, (w, b) in enumerate(weights):
-        twin_w[i].wait_recv()
-        far_core_w.append(send(b.at[2], b.at[3], core))
-    for i in range(2):
+
+    def forward_s(i):
         over_s[i].wait_recv()
         block = part(grads, cap + i * step, step)
         near_s.append(send(block, part(grads, slots + cap + i * step, step), near))
 
-    for copy in own_w + own_r:
-        copy.wait()
-    for copy in near_x + core_w + far_core_w:
-        copy.wait_recv()
-
-    for q in range(2):
+    def activation(q):
         columns = slice(q * quarter, (q + 1) * quarter)
         left, right = rows[:, :half], rows[:, half:]
         g = dot(left, gates_w[2 * q], 1, 0) + dot(right, gates_w[2 * q + 1], 1, 0)
@@ -122,6 +114,22 @@
         g_buf[:, columns] = g
         u_buf[:, columns] = u
         act[:, columns] = (g * jax.nn.sigmoid(g) * u).astype(BF16)
+
+    forward_s(0)
+    for copy in own_w + own_r:
+        copy.wait()
+    for copy in near_x + core_w:
+        copy.wait_recv()
+    activation(0)
+    far_core_w = []
+    for i, (w, b) in enumerate(weights):
+        twin_w[i].wait_recv()
+        far_core_w.append(send(b.at[2], b.at[3], core))
+    forward_s(1)
+    for copy in far_core_w[:2]:
+        copy.wait_recv()
+    activation(1)
+    far_core_w[2].wait_recv()
 
     tile = half // 2
 
@@ -181,6 +189,22 @@
     core_g = [send(tg.at[q], rg.at[q], core) for q in (1, 0)]
     core_u = [send(tu.at[q], ru.at[q], core) for q in (1, 0)]
 
+    homeward = []
+    places = (cap, cap + step, 0, step)
+
+    def finish(keep, arrived, copies, result, which):
+        for i in which:
+            at = places[i]
+            copies[i].wait_recv()
+            total = keep[at : at + step].astype(F32) + arrived[at : at + step].astype(F32)
+            keep[at : at + step] = total.astype(BF16)
+            if at >= cap:
+                homeward.append(send(part(keep, at, step), part(result, at, step), home))
+            else:
+                local(part(keep, at, step), part(result, at, step))
+
+    finish(out_keep, out_recv, near_out, bo, (0, 1))
+
     for copy in core_d:
         copy.wait_recv()
 
@@ -192,6 +216,14 @@
         zsd[:, pl.ds(at, tile)] = (value[quarter:] + rd[1, :, pl.ds(at, tile)].astype(F32)).astype(BF16)
 
     far_d = send(zsd, zrd, far)
+
+    def make_dx(h, columns):
+        value = dot(dd[:, :quarter], gates_w[h, columns], 1, 1)
+        value = value + dot(dd[:, quarter : 2 * quarter], gates_w[2 + h, columns], 1, 1)
+        value = value + dot(dd[:, 2 * quarter : 3 * quarter], ups_w[h, columns], 1, 1)
+        return value + dot(dd[:, 3 * quarter :], ups_w[2 + h, columns], 1, 1)
+
+    near_dx = give(dx_keep, dx_send, dx_recv, make_dx)
 
     for copy in core_g + core_u:
         copy.wait_recv()
@@ -209,26 +241,9 @@
     far_g = send(zsg, zrg, far)
     far_u = send(zsu, zru, far)
 
-    def make_dx(h, columns):
-        value = dot(dd[:, :quarter], gates_w[h, columns], 1, 1)
-        value = value + dot(dd[:, quarter : 2 * quarter], gates_w[2 + h, columns], 1, 1)
-        value = value + dot(dd[:, 2 * quarter : 3 * quarter], ups_w[h, columns], 1, 1)
-        return value + dot(dd[:, 3 * quarter :], ups_w[2 + h, columns], 1, 1)
-
-    near_dx = give(dx_keep, dx_send, dx_recv, make_dx)
-
-    homeward = []
-    for keep, arrived, copies, result in (
-        (out_keep, out_recv, near_out, bo), (dx_keep, dx_recv, near_dx, bx),
-    ):
-        for copy, at in zip(copies, (cap, cap + step, 0, step)):
-            copy.wait_recv()
-            total = keep[at : at + step].astype(F32) + arrived[at : at + step].astype(F32)
-            keep[at : at + step] = total.astype(BF16)
-            if at >= cap:
-                homeward.append(send(part(keep, at, step), part(result, at, step), home))
-            else:
-                local(part(keep, at, step), part(result, at, step))
+    finish(dx_keep, dx_recv, near_dx, bx, (0, 1))
+    finish(out_keep, out_recv, near_out, bo, (2, 3))
+    finish(dx_keep, dx_recv, near_dx, bx, (2, 3))
 
     for copy, mine, got in ((far_d, od, zrd), (far_g, og, zrg), (far_u, ou, zru)):
         copy.wait_recv()

time: 218 us -> 208 us (0.954)
  Pallas kernels: 200 us -> 190 us
    pallas_call x1, Pallas kernels: 200 us -> 190 us  [layer(): pl.pallas_call(functools.partial(layer_kernel, cap, half, quarter), out_s...]
where the time goes in v3:
time: 208 us; the launch traced here: 207 us
  Pallas kernels  190 us (91%)
  matrix products  5.99 us (3%)
  other arithmetic  5.65 us (3%)
  local copies, waits for them, and re-layouts  4.73 us (2%)
    pallas_call x1, Pallas kernels, layer(): pl.pallas_call(functools.partial(layer_kernel, cap, half, quarter), out_s...  190 us
    dot_general x5, matrix products, dot(): lax.dot_general(a, b, (((ca,), (cb,)), ((), ())), preferred_element_type=...  5.99 us
    unnamed x17, local copies, waits for them, and re-layouts  4.42 us

profile of v3, /device:TPU:8, one launch (start us, length us, event | category | flops | bytes accessed | tf_op | source)
XLA Modules:
  0.0 207.3 jit_solution(9945016177328997804)
XLA Ops:
  1.3 0.7 fusion.20
  2.0 0.1 fusion.3
  2.1 0.7 fusion.16
  2.8 1.4 fusion
  4.2 0.1 fusion.23
  4.3 0.0 copy-start.1
  4.3 1.7 convolution_convert_fusion.ps
  6.0 0.0 copy-done.1
  6.0 0.1 fusion.24
  6.1 1.8 convolution_convert_fusion.1.px
  7.8 189.5 %shard_map.127 = (bf16[192,3584]{1,0:T(8,128)(2,1)}, bf16[192,3584]{1,0:T(8,128)(2,1)}, bf16[1792,256]{1,0:T(8,128)(2,1)}, bf16[1792,256]{1,0:T(8,128)(2,1)}, bf16[256,1792]{1,0:T(8,128)(2,1)}) custom-call(bf16[192,3584]{1,0:T(8,128)(2,1)} %convolution_convert_fusion.1.px, bf16[192,3584]{1,0:T(8,128)(2,1)} %convolution_convert_fusion.ps, ...), custom_call_target="tpu_custom_call" | custom-call | flops 12683575296 | bytes 36700160 | tf_op jit(solution)/shard_map/pallas_call | solution.py:271
  197.4 0.0 copy-start.2
  197.4 1.9 fusion.11
  199.3 0.0 copy-done.2
  199.3 0.5 fusion.10
  199.8 0.1 fusion.22
  199.8 1.1 fusion.2
  201.0 0.0 copy-start
  201.0 0.0 copy-start.6
  201.0 0.1 fusion.21
  201.1 1.1 copy-done
  202.1 0.0 copy-done.6
  202.1 0.0 copy-start.5
  202.1 1.8 fusion.1
  203.9 0.0 copy-start.4
  203.9 0.0 copy-done.5
  203.9 0.0 copy-start.3
  203.9 0.9 copy.18
  204.8 0.6 copy-done.4
  205.4 0.9 copy.19
  206.3 0.0 copy-done.3
  206.4 0.9 copy.20
Async XLA Ops:
  4.3 1.7 copy-start.1
  197.4 1.9 copy-start.2
  201.0 1.2 copy-start
  201.0 1.2 copy-start.6
  202.1 1.8 copy-start.5
  203.9 1.5 copy-start.4
  203.9 2.4 %copy-start.3 = (bf16[256,1792]{1,0:T(8,128)(2,1)S(1)}, bf16[256,1792]{1,0:T(8,128)(2,1)}, u32[]{:S(2)}) copy-start(bf16[256,1792]{1,0:T(8,128)(2,1)} %get-tuple-element.15) | copy-start | bytes 2752516

commit v4 on v3

--- a/solution.py
+++ b/solution.py
@@ -23,10 +23,10 @@
 def layer_kernel(
     cap, half, quarter,
     px, ps, wg, wu, wd,
-    bo, bx, og, ou, od,
+    bo, bx, og, ou, od, zrg, zru, zrd,
     rows, grads, gates_w, ups_w, downs_w, g_buf, u_buf, act, dd,
     out_keep, out_send, out_recv, dx_keep, dx_send, dx_recv,
-    tg, tu, td, rg, ru, rd, zsg, zsu, zsd, zrg, zru, zrd,
+    tg, tu, td, rg, ru, rd, zsg, zsu, zsd,
     send_sem, recv_sem, local_sem,
 ):
     me, group = lax.axis_index("expert"), lax.axis_index("groups")
@@ -74,10 +74,6 @@
         send(part(px, cap + i * step, step), part(rows, cap + i * step, step), home)
         for i in range(2)
     ]
-    over_s = [
-        send(part(ps, cap + i * step, step), part(grads, cap + i * step, step), home)
-        for i in range(2)
-    ]
     near_x = [send(part(px, 0, cap), part(rows, slots, cap), near)]
     near_s = [send(part(ps, 0, cap), part(grads, slots, cap), near)]
     weights = ((wg, gates_w), (wu, ups_w), (wd, downs_w))
@@ -86,19 +82,27 @@
         size = ref.shape[0] // 2
         return ref.at[pl.ds(pl.multiple_of(which * size, size), size)]
 
-    far_w = [send(group_half(w, group), group_half(b.at[2], group), far) for w, b in weights]
+    far_w = [
+        send(group_half(w, group), group_half(b.at[2], group), far) for w, b in weights[:2]
+    ]
     core_w = [send(w, b.at[1], core) for w, b in weights]
     own_w = [local(w, b.at[0]) for w, b in weights]
     own_r = [local(part(px, 0, cap), part(rows, 0, cap)),
              local(part(ps, 0, cap), part(grads, 0, cap))]
 
+    over_s = []
     for i in range(2):
         over_x[i].wait_recv()
+        over_s.append(
+            send(part(ps, cap + i * step, step), part(grads, cap + i * step, step), home)
+        )
         block = part(rows, cap + i * step, step)
         near_x.append(send(block, part(rows, slots + cap + i * step, step), near))
     twin_w = []
     for i, (w, b) in enumerate(weights):
         far_w[i].wait_recv()
+        if i == 0:
+            far_w.append(send(group_half(wd, group), group_half(downs_w.at[2], group), far))
         twin_w.append(send(group_half(b.at[2], group), group_half(b.at[2], group), twin))
 
     def forward_s(i):
@@ -144,7 +148,7 @@
                 away[:, columns] = value[slots:]
         return [
             send(part(away, at, step), part(arrived, at, step), near)
-            for at in (cap, cap + step, 0, step)
+            for at in (cap, cap + step)
         ]
 
     def make_out(h, columns):
@@ -192,18 +196,20 @@
     homeward = []
     places = (cap, cap + step, 0, step)
 
-    def finish(keep, arrived, copies, result, which):
+    def finish(keep, away, arrived, copies, result, which):
         for i in which:
             at = places[i]
             copies[i].wait_recv()
             total = keep[at : at + step].astype(F32) + arrived[at : at + step].astype(F32)
             keep[at : at + step] = total.astype(BF16)
             if at >= cap:
+                later = places[i + 2]
                 homeward.append(send(part(keep, at, step), part(result, at, step), home))
+                copies.append(send(part(away, later, step), part(arrived, later, step), near))
             else:
                 local(part(keep, at, step), part(result, at, step))
 
-    finish(out_keep, out_recv, near_out, bo, (0, 1))
+    finish(out_keep, out_send, out_recv, near_out, bo, (0, 1))
 
     for copy in core_d:
         copy.wait_recv()
@@ -241,13 +247,12 @@
     far_g = send(zsg, zrg, far)
     far_u = send(zsu, zru, far)
 
-    finish(dx_keep, dx_recv, near_dx, bx, (0, 1))
-    finish(out_keep, out_recv, near_out, bo, (2, 3))
-    finish(dx_keep, dx_recv, near_dx, bx, (2, 3))
-
-    for copy, mine, got in ((far_d, od, zrd), (far_g, og, zrg), (far_u, ou, zru)):
-        copy.wait_recv()
-        mine[...] = (mine[...].astype(F32) + got[...].astype(F32)).astype(BF16)
+    finish(dx_keep, dx_send, dx_recv, near_dx, bx, (0, 1))
+    finish(out_keep, out_send, out_recv, near_out, bo, (2, 3))
+    finish(dx_keep, dx_send, dx_recv, near_dx, bx, (2, 3))
+
+    for copy in (far_d, far_g, far_u):
+        copy.wait_recv()
     for copy in homeward:
         copy.wait_recv()
     for copy in locals_[len(own_w + own_r):]:
@@ -268,11 +273,11 @@
     inside = pl.BlockSpec(memory_space=pltpu.VMEM)
     ff = 2 * quarter
     copies = 43
-    return pl.pallas_call(
+    back_out, back_dx, *sums = pl.pallas_call(
         functools.partial(layer_kernel, cap, half, quarter),
-        out_shape=(back, back, like(wg), like(wu), like(wd)),
+        out_shape=(back, back) + (like(wg), like(wu), like(wd)) * 2,
         in_specs=[anywhere] * 5,
-        out_specs=(anywhere, anywhere, inside, inside, inside),
+        out_specs=(anywhere,) * 2 + (inside,) * 3 + (anywhere,) * 3,
         scratch_shapes=[
             vmem(count, width), vmem(count, width),
             vmem(4, half, quarter), vmem(4, half, quarter), vmem(4, quarter, half),
@@ -281,7 +286,7 @@
         ]
         + [vmem(slots, width)] * 6
         + [vmem(2, half, quarter), vmem(2, half, quarter), vmem(2, quarter, half)] * 2
-        + [vmem(half, quarter), vmem(half, quarter), vmem(quarter, half)] * 2
+        + [vmem(half, quarter), vmem(half, quarter), vmem(quarter, half)]
         + [
             pltpu.SemaphoreType.DMA((copies,)),
             pltpu.SemaphoreType.DMA((copies,)),
@@ -295,6 +300,8 @@
             transcendentals=2 * count * ff,
         ),
     )(packed_x, packed_s, wg, wu, wd)
+    added = [(a.astype(F32) + b.astype(F32)).astype(BF16) for a, b in zip(sums[:3], sums[3:])]
+    return back_out, back_dx, *added
 
 
 def layer_by_permutes(experts, capacity, packed_x, packed_s, w_gate, w_up, w_down):

time: 208 us -> 209 us (level); the launches traced: 207 us -> 205 us
  Pallas kernels: 190 us -> 187 us
  other arithmetic: 5.65 us -> 8.54 us
    pallas_call x1, Pallas kernels: 190 us -> 187 us  [layer(): pl.pallas_call(functools.partial(layer_kernel, cap, half, quarter), out_s...]
    broadcast_in_dim x0 -> x2, other arithmetic: none -> 2.88 us  [the longest x1 1.75 us: on_device(): grad_wg[None]]
    unnamed x17 -> x20, local copies, waits for them, and re-layouts: 4.42 us -> 2.6 us
where the time goes in v4:
time: 209 us; the launch traced here: 205 us
  Pallas kernels  187 us (89%)
  other arithmetic  8.54 us (4%)
  matrix products  5.97 us (3%)
  local copies, waits for them, and re-layouts  2.9 us (1%)
    pallas_call x1, Pallas kernels, layer(): pl.pallas_call(functools.partial(layer_kernel, cap, half, quarter), out_s...  187 us
    dot_general x5, matrix products, dot(): lax.dot_general(a, b, (((ca,), (cb,)), ((), ())), preferred_element_type=...  5.97 us

profile of v4, /device:TPU:8, one launch (start us, length us, event | category | flops | bytes accessed | tf_op | source)
XLA Modules:
  0.0 205.3 jit_solution(16400041380899773864)
XLA Ops:
  1.3 0.7 fusion.23
  2.0 0.1 fusion.3
  2.1 0.7 fusion.19
  2.8 1.4 fusion
  4.2 0.1 fusion.26
  4.3 0.0 copy-start.1
  4.3 1.7 convolution_convert_fusion.ps
  6.0 0.0 copy-done.1
  6.0 0.1 fusion.27
  6.1 1.7 convolution_convert_fusion.1.px
  7.8 186.5 %shard_map.127 = (bf16[192,3584]{1,0:T(8,128)(2,1)}, bf16[192,3584]{1,0:T(8,128)(2,1)}, bf16[1792,256]{1,0:T(8,128)(2,1)}, bf16[1792,256]{1,0:T(8,128)(2,1)}, bf...) custom-call(bf16[192,3584]{1,0:T(8,128)(2,1)} %convolution_convert_f, ...), custom_call_target="tpu_custom_call" | custom-call | flops 12683575296 | bytes 36700160 | tf_op jit(solution)/shard_map/pallas_call | solution.py:276
  194.3 0.0 copy-start.2
  194.4 1.9 fusion.14
  196.3 0.0 copy-done.2
  196.3 0.0 copy-start.7
  196.3 0.0 copy-start.8
  196.3 0.5 fusion.13
  196.7 0.7 copy-done.7
  197.4 0.3 copy-done.8
  197.7 1.1 fusion.6
  198.9 0.1 fusion.25
  198.9 1.1 fusion.2
  200.1 0.1 fusion.24
  200.2 1.1 copy-done
  201.2 0.0 copy-done.9
  201.2 0.0 copy-start.6
  201.3 1.8 fusion.1
  203.0 0.0 copy-done.3
  203.0 0.0 copy-done.4
  203.0 0.3 copy-done.5
  203.3 0.3 copy-done.6
  203.6 1.7 fusion.4
  (5 shorter events, 0.0 us)
Async XLA Ops:
  4.3 1.7 copy-start.1
  194.3 1.9 copy-start.2
  196.3 1.2 copy-start.7
  196.3 1.4 copy-start.8
  200.1 1.2 copy-start
  200.1 1.2 copy-start.9
  201.2 1.8 copy-start.3
  201.2 1.8 copy-start.4
  201.2 2.1 %copy-start.5 = (bf16[1792,256]{1,0:T(8,128)(2,1)S(1)}, bf16[1792,256]{1,0:T(8,128)(2,1)}, u32[]{:S(2)}) copy-start(bf16[1792,256]{1,0:T(8,128)(2,1)} %get-tuple-element.17) | copy-start | bytes 2752516
  201.2 2.3 %copy-start.6 = (bf16[1792,256]{1,0:T(8,128)(2,1)S(1)}, bf16[1792,256]{1,0:T(8,128)(2,1)}, u32[]{:S(2)}) copy-start(bf16[1792,256]{1,0:T(8,128)(2,1)} %get-tuple-element.19) | copy-start | bytes 2752516

commit v5 on v3

--- a/solution.py
+++ b/solution.py
@@ -74,10 +74,6 @@
         send(part(px, cap + i * step, step), part(rows, cap + i * step, step), home)
         for i in range(2)
     ]
-    over_s = [
-        send(part(ps, cap + i * step, step), part(grads, cap + i * step, step), home)
-        for i in range(2)
-    ]
     near_x = [send(part(px, 0, cap), part(rows, slots, cap), near)]
     near_s = [send(part(ps, 0, cap), part(grads, slots, cap), near)]
     weights = ((wg, gates_w), (wu, ups_w), (wd, downs_w))
@@ -92,8 +88,12 @@
     own_r = [local(part(px, 0, cap), part(rows, 0, cap)),
              local(part(ps, 0, cap), part(grads, 0, cap))]
 
+    over_s = []
     for i in range(2):
         over_x[i].wait_recv()
+        over_s.append(
+            send(part(ps, cap + i * step, step), part(grads, cap + i * step, step), home)
+        )
         block = part(rows, cap + i * step, step)
         near_x.append(send(block, part(rows, slots + cap + i * step, step), near))
     twin_w = []

time: 208 us -> 201 us (0.966)
  Pallas kernels: 190 us -> 182 us
    pallas_call x1, Pallas kernels: 190 us -> 182 us  [layer(): pl.pallas_call(functools.partial(layer_kernel, cap, half, quarter), out_s...]
where the time goes in v5:
time: 201 us; the launch traced here: 200 us
  Pallas kernels  182 us (91%)
  matrix products  5.99 us (3%)
  other arithmetic  5.65 us (3%)
  local copies, waits for them, and re-layouts  4.73 us (2%)
    pallas_call x1, Pallas kernels, layer(): pl.pallas_call(functools.partial(layer_kernel, cap, half, quarter), out_s...  182 us
    dot_general x5, matrix products, dot(): lax.dot_general(a, b, (((ca,), (cb,)), ((), ())), preferred_element_type=...  5.99 us
    unnamed x17, local copies, waits for them, and re-layouts  4.42 us

profile of v5, /device:TPU:8, one launch (start us, length us, event | category | flops | bytes accessed | tf_op | source)
XLA Modules:
  0.0 200.0 jit_solution(549631775437525295)
XLA Ops:
  1.3 0.7 fusion.20
  2.0 0.1 fusion.3
  2.1 0.7 fusion.16
  2.8 1.4 fusion
  4.2 0.1 fusion.23
  4.3 0.0 copy-start.1
  4.3 1.7 convolution_convert_fusion.ps
  6.0 0.0 copy-done.1
  6.0 0.1 fusion.24
  6.1 1.8 convolution_convert_fusion.1.px
  7.8 182.2 %shard_map.127 = (bf16[192,3584]{1,0:T(8,128)(2,1)}, bf16[192,3584]{1,0:T(8,128)(2,1)}, bf16[1792,256]{1,0:T(8,128)(2,1)}, bf16[1792,256]{1,0:T(8,128)(2,1)}, bf16[256,1792]{1,0:T(8,128)(2,1)}) custom-call(bf16[192,3584]{1,0:T(8,128)(2,1)} %convolution_convert_fusion.1.px, bf16[192,3584]{1,0:T(8,128)(2,1)} %convolution_convert_fusion.ps, ...), custom_call_target="tpu_custom_call" | custom-call | flops 12683575296 | bytes 36700160 | tf_op jit(solution)/shard_map/pallas_call | solution.py:271
  190.1 0.0 copy-start.2
  190.1 1.9 fusion.11
  192.0 0.0 copy-done.2
  192.0 0.5 fusion.10
  192.5 0.1 fusion.22
  192.5 1.1 fusion.2
  193.7 0.0 copy-start
  193.7 0.0 copy-start.6
  193.7 0.1 fusion.21
  193.8 1.1 copy-done
  194.8 0.0 copy-done.6
  194.8 0.0 copy-start.5
  194.8 1.8 fusion.1
  196.6 0.0 copy-start.4
  196.6 0.0 copy-done.5
  196.6 0.0 copy-start.3
  196.6 0.9 copy.18
  197.6 0.6 copy-done.4
  198.1 0.9 copy.19
  199.1 0.0 copy-done.3
  199.1 0.9 copy.20
Async XLA Ops:
  4.3 1.7 copy-start.1
  190.1 1.9 copy-start.2
  193.7 1.2 copy-start
  193.7 1.2 copy-start.6
  194.8 1.8 copy-start.5
  196.6 1.5 copy-start.4
  196.6 2.4 %copy-start.3 = (bf16[256,1792]{1,0:T(8,128)(2,1)S(1)}, bf16[256,1792]{1,0:T(8,128)(2,1)}, u32[]{:S(2)}) copy-start(bf16[256,1792]{1,0:T(8,128)(2,1)} %get-tuple-element.15) | copy-start | bytes 2752516
